TPU v7x, 256 devices: a whole 4x4x8 slice. The times are simulated.
256 devices in a mesh: gx: 32 (over z, x), gy: 8 (over y, core).
Axes of the slice: x: 4, y: 4, z: 8, core: 2. Of those that a mesh axis runs over, the one named last changes fastest.
Arguments:
- source_field: float32 [3, 8, 128, 64, 128], P(None, None, 'gx', 'gy'), may hold values from -50 to 50
- density_class: int32 [128, 64, 128], P('gx', 'gy'), may hold values from 0 to 15
- fixed_mask: int32 [128, 64, 128], P('gx', 'gy'), may hold values 0 or 1
- load_nodes: int32 [8, 64], replicated, may hold values from 0 to 1048575, as said below
- load_forces: float32 [3, 8, 64], replicated, may hold values from -16 to 16
Outputs:
- solution: float32 [3, 8, 128, 64, 128], P(None, None, 'gx', 'gy')
- residual: float32 [3, 8, 128, 64, 128], P(None, None, 'gx', 'gy')
Inputs may be any that keep to these rules, and one draw needn't show every extreme that they name: `load_nodes`: each entry is the index (x * 64 + y) * 128 + z of a voxel of the whole grid; repeats may occur.
All inputs are finite; a program needn't handle non-finite values. No bound on the sum of `fixed_mask` on one device may be relied on, other than what follows from the above.
Results may differ from a plain program's by a relative error of at most 0.0003.
Values sent between devices are 32-bit elements; how exact they have to be, the bound alone decides.
A program may use at most 128 MiB of HBM per device.

v0:
```python
import math

import jax
import jax.numpy as jnp
from jax import lax
from jax.sharding import PartitionSpec as P

CLASSES = 16
LEVELS = 3
ITERS = 2


SHEAR_MODULUS = 1.0 / 2.6
LAME_FIRST = 0.3 / 0.52
MIN_MODULUS = 0.05
STEP_FIRST = 1.0 / (2.7 + 2.1 * math.cos(math.pi / 4.0))
STEP_SECOND = 1.0 / (2.7 - 2.1 * math.cos(math.pi / 4.0))


def padded_2(block, sides, width):
    for axis, dim in sides:
        count = lax.axis_size(axis)
        forward = [(i, i + 1) for i in range(count - 1)]
        backward = [(target, source) for source, target in forward]
        low = lax.ppermute(
            lax.slice_in_dim(block, block.shape[dim] - width, None, axis=dim), axis, forward
        )
        high = lax.ppermute(lax.slice_in_dim(block, 0, width, axis=dim), axis, backward)
        block = jnp.concatenate([low, block, high], axis=dim)
    return block


def crop_box(array, starts, lengths):
    return array[
        ...,
        starts[0] : starts[0] + lengths[0],
        starts[1] : starts[1] + lengths[1],
        starts[2] : starts[2] + lengths[2],
    ]


def offset_along(axis_d, moved, rest):
    return tuple((moved if k == axis_d else rest for k in range(3)))


def stiffness(padded, modulus):
    shape_now = padded.shape[-3:]
    inside_len = tuple((s - 2 for s in shape_now))
    outer_len = tuple((s - 1 for s in shape_now))
    middle = crop_box(padded, (1, 1, 1), inside_len)
    middle_mod = crop_box(modulus, (1, 1, 1), inside_len)
    laplacian = jnp.zeros_like(middle)
    for d in range(3):
        lower_box = offset_along(d, 0, 1)
        upper_box = offset_along(d, 2, 1)
        laplacian = laplacian + (crop_box(modulus, lower_box, inside_len) + middle_mod) * (
            middle - crop_box(padded, lower_box, inside_len)
        )
        laplacian = laplacian + (middle_mod + crop_box(modulus, upper_box, inside_len)) * (
            middle - crop_box(padded, upper_box, inside_len)
        )
    spread_sum = crop_box(padded[0], (1, 0, 0), outer_len) - crop_box(
        padded[0], (0, 0, 0), outer_len
    )
    for d in (1, 2):
        spread_sum = (
            spread_sum
            + crop_box(padded[d], offset_along(d, 1, 0), outer_len)
            - crop_box(padded[d], (0, 0, 0), outer_len)
        )
    flux_field = LAME_FIRST * crop_box(modulus, (0, 0, 0), outer_len) * spread_sum
    pieces = [
        crop_box(flux_field, offset_along(c, 0, 1), inside_len)
        - crop_box(flux_field, (1, 1, 1), inside_len)
        for c in range(3)
    ]
    return 0.5 * SHEAR_MODULUS * laplacian + jnp.stack(pieces)


def diagonal_inverse(modpad, free):
    inside_len = tuple((s - 2 for s in modpad.shape))
    middle_mod = crop_box(modpad, (1, 1, 1), inside_len)
    total = jnp.zeros_like(middle_mod)
    for d in range(3):
        total = (
            total
            + crop_box(modpad, offset_along(d, 0, 1), inside_len)
            + 2.0 * middle_mod
            + crop_box(modpad, offset_along(d, 2, 1), inside_len)
        )
    rows = [
        0.5 * SHEAR_MODULUS * total
        + LAME_FIRST * (middle_mod + crop_box(modpad, offset_along(c, 0, 1), inside_len))
        for c in range(3)
    ]
    diagonal = jnp.stack(rows)
    return (free / diagonal + (1.0 - free))[:, None]


def restrict_sum(field):
    lead = field.shape[:-3]
    extent = field.shape[-3:]
    shaped = field.reshape(lead + (extent[0] // 2, 2, extent[1] // 2, 2, extent[2] // 2, 2))
    return jnp.sum(shaped, axis=(-5, -3, -1))


def prolong(field):
    lead = field.shape[:-3]
    extent = field.shape[-3:]
    expanded = field[..., :, None, :, None, :, None]
    wide = jnp.broadcast_to(expanded, lead + (extent[0], 2, extent[1], 2, extent[2], 2))
    return wide.reshape(lead + (2 * extent[0], 2 * extent[1], 2 * extent[2]))


def modulus_rim(modulus):
    padded = padded_2(modulus, (("gx", 0), ("gy", 1)), 1)
    return jnp.pad(padded, ((0, 0), (0, 0), (1, 1)))


def apply_level(field, section):
    modpad, free, dinv = section
    padded = padded_2(free * field, (("gx", 2), ("gy", 3)), 1)
    padded = jnp.pad(padded, ((0, 0), (0, 0), (0, 0), (0, 0), (1, 1)))
    return free * stiffness(padded, modpad) + (1.0 - free) * field


def plain_presmooth(rhs, section):
    dinv = section[2]
    current = STEP_FIRST * dinv * rhs
    remain = rhs - apply_level(current, section)
    current = current + STEP_SECOND * dinv * remain
    remain = rhs - apply_level(current, section)
    return (current, remain)


def vcycle(rhs, levels, level, presmooth):
    section = levels[level]
    dinv = section[2]
    if level == len(levels) - 1:
        current = STEP_FIRST * dinv * rhs
        return current + STEP_SECOND * dinv * (rhs - apply_level(current, section))
    if level == 0:
        current, remain = presmooth(rhs, section)
    else:
        current, remain = plain_presmooth(rhs, section)
    coarse = vcycle(restrict_sum(remain), levels, level + 1, presmooth)
    current = current + section[1] * prolong(coarse)
    current = current + STEP_SECOND * dinv * (rhs - apply_level(current, section))
    current = current + STEP_FIRST * dinv * (rhs - apply_level(current, section))
    return current


def gram_matrix(left, right):
    return jnp.einsum("cixyz,cjxyz->ij", left, right, precision=lax.Precision.HIGHEST)


def combine_cases(field, matrix):
    return jnp.einsum("cixyz,ij->cjxyz", field, matrix, precision=lax.Precision.HIGHEST)


def solve_small(matrix, rhs):
    factor = jnp.linalg.cholesky(matrix)
    middle = lax.linalg.triangular_solve(factor, rhs, left_side=True, lower=True)
    return lax.linalg.triangular_solve(factor, middle, left_side=True, lower=True, transpose_a=True)


def residual_gram(residual, precond):
    return lax.psum(gram_matrix(residual, precond), ("gx", "gy"))


def on_device(source_field, density_class, fixed_mask, load_nodes, load_forces):
    cases = source_field.shape[1]
    cells_x, cells_y, cells_z = source_field.shape[-3:]
    relative = (density_class.astype(jnp.float32) + 1.0) / CLASSES
    modulus = MIN_MODULUS + (1.0 - MIN_MODULUS) * relative * relative * relative
    free = 1.0 - fixed_mask.astype(jnp.float32)
    levels = []
    for level in range(LEVELS):
        if level > 0:
            modulus = 0.25 * restrict_sum(modulus)
            free = jnp.ones_like(modulus)
        modpad = modulus_rim(modulus)
        levels.append((modpad, free, diagonal_inverse(modpad, free)))

    def presmooth(rhs, section):
        return plain_presmooth(rhs, section)

    flat = source_field.reshape(3, cases, -1)
    rows_y = cells_y * lax.axis_size("gy")
    plane = rows_y * cells_z
    coord_x = load_nodes // plane
    coord_y = load_nodes // cells_z % rows_y
    coord_z = load_nodes % cells_z
    local_x = coord_x - lax.axis_index("gx") * cells_x
    local_y = coord_y - lax.axis_index("gy") * cells_y
    inside = (local_x >= 0) & (local_x < cells_x) & (local_y >= 0) & (local_y < cells_y)
    local_node = jnp.where(
        inside, (local_x * cells_y + local_y) * cells_z + coord_z, cells_x * cells_y * cells_z
    )
    case_ids = jnp.broadcast_to(jnp.arange(cases, dtype=jnp.int32)[:, None], load_nodes.shape)
    flat = flat.at[:, case_ids, local_node].add(load_forces, mode="drop")
    right = levels[0][1] * flat.reshape(source_field.shape)
    solution = jnp.zeros_like(right)
    residual = right
    precond = vcycle(residual, levels, 0, presmooth)
    search = precond
    rz_gram = residual_gram(residual, precond)
    for step in range(ITERS):
        image = apply_level(search, levels[0])
        pq_gram = lax.psum(gram_matrix(search, image), ("gx", "gy"))
        alpha = solve_small(pq_gram, rz_gram)
        solution = solution + combine_cases(search, alpha)
        residual = residual - combine_cases(image, alpha)
        if step + 1 < ITERS:
            precond = vcycle(residual, levels, 0, presmooth)
            rz_next = residual_gram(residual, precond)
            beta = solve_small(rz_gram, rz_next)
            search = precond + combine_cases(search, beta)
            rz_gram = rz_next
    return (solution, residual)


def solution(mesh):
    placed = (P(None, None, "gx", "gy", None), P("gx", "gy", None), P("gx", "gy", None), P(), P())
    return jax.shard_map(
        on_device,
        mesh=mesh,
        in_specs=placed,
        out_specs=(P(None, None, "gx", "gy", None), P(None, None, "gx", "gy", None)),
        check_vma=False,
    )
```

profile of v0, /device:TPU:1, one launch (start us, length us, event | category | flops | bytes accessed | tf_op | source)
XLA Modules:
  0.0 805.2 jit_solution(845960222873638603)
XLA Ops:
  16.2 4.6 collective-permute-start.11
  24.0 8.7 %copy.476 = f32[3,8,4,8,128]{0,4,3,2,1:T(8,128)} copy(f32[3,8,4,8,128]{4,3,2,1,0:T(8,128)S(1)} %copy-done) | data formatting | bytes 786432 | tf_op args[0]
  32.9 49.7 %scatter_fusion = f32[3,8,4096]{0,2,1:T(8,128)} fusion(f32[3,8,4096]{0,2,1:T(8,128)} %bitcast.437, s32[512]{0:T(512)S(1)} %reshape.347, f32[512,3]{1,0:T(8,128)S(1)} %bitcast.447), kind=kCustom, calls=%fused_computation | custom fusion | flops 1536 | bytes 22528 | tf_op jit(solution)/shard_map/scatter-add | solution.py:201
  82.6 10.0 %copy.479 = f32[3,8,4,8,128]{4,1,3,2,0:T(8,128)S(1)} copy(f32[3,8,4,8,128]{0,4,3,2,1:T(8,128)} %bitcast.438) | data formatting | bytes 786432 | tf_op jit(solution)/shard_map/reshape | solution.py:202
  107.2 4.4 collective-permute-start.4
  113.5 4.5 collective-permute-start.22
  127.7 6.8 collective-permute-start.12
  138.0 5.5 collective-permute-start.14
  150.2 6.8 reduce_sum.66
  158.5 6.1 collective-permute-start.16
  167.7 5.3 collective-permute-start.18
  175.8 6.4 collective-permute-start.24
  185.3 5.1 collective-permute-start.26
  194.0 6.3 collective-permute-start.28
  203.1 5.1 collective-permute-start.30
  211.4 6.8 collective-permute-start.32
  221.3 5.1 collective-permute-start.34
  229.3 6.7 collective-permute-start.36
  239.1 5.1 collective-permute-start.38
  246.2 5.7 broadcast_in_dim.35
  251.9 4.3 copy.491
  257.6 6.7 collective-permute-start.40
  267.9 5.2 collective-permute-start.42
  277.2 6.7 collective-permute-start.44
  287.5 5.1 collective-permute-start.46
  296.7 6.7 collective-permute-start.48
  307.0 5.1 collective-permute-start.50
  315.8 105.9 %all-reduce.23 = (f32[8,8]{0,1:T(8,128)S(1)}, f32[8,8]{0,1:T(8,128)S(1)}) all-reduce(f32[8,8]{0,1:T(8,128)S(1)} %convolution_bitcast_fusion.8, f32[8,8]{0,1:T(8,128)S(1)} %convolution_bitcast_fusion.9), channel_id=1, replica_groups=mesh['gx'=32,'gy'=8] {'gx','gy'}, use_global_device_ids=true, to_apply=%region_10.12 | all-reduce | flops 128 | bytes 1024 | tf_op jit(solution)/shard_map/psum | solution.py:168
  442.5 4.7 collective-permute-start.56
  462.5 6.8 reduce_sum.88
  470.9 4.7 collective-permute-start.60
  478.7 5.1 collective-permute-start.62
  486.8 4.6 collective-permute-start.64
  494.5 5.1 collective-permute-start.66
  503.1 4.8 collective-permute-start.68
  510.7 5.1 collective-permute-start.70
  519.0 6.8 collective-permute-start.72
  528.9 5.3 collective-permute-start.74
  536.9 6.7 collective-permute-start.76
  546.7 5.1 collective-permute-start.78
  553.8 5.7 broadcast_in_dim.40
  559.5 4.3 copy.510
  565.2 6.7 collective-permute-start.80
  575.5 5.1 collective-permute-start.82
  584.7 6.7 collective-permute-start.84
  594.9 5.1 collective-permute-start.86
  603.8 97.9 %psum.30 = f32[8,8]{1,0:T(8,128)S(1)} all-reduce(f32[8,8]{1,0:T(8,128)S(1)} %convolution_bitcast_fusion.6), channel_id=1, replica_groups=mesh['gx'=32,'gy'=8] {'gx','gy'}, use_global_device_ids=true, to_apply=%region_14.18 | all-reduce | flops 64 | bytes 512 | tf_op jit(solution)/shard_map/psum | solution.py:168
  719.2 80.1 %psum.31 = f32[8,8]{0,1:T(8,128)S(1)} all-reduce(f32[8,8]{0,1:T(8,128)S(1)} %convolution_bitcast_fusion.4), channel_id=1, replica_groups=mesh['gx'=32,'gy'=8] {'gx','gy'}, use_global_device_ids=true, to_apply=%region_15.19 | all-reduce | flops 64 | bytes 512 | tf_op jit(solution)/shard_map/psum | solution.py:210
  (396 shorter events, 215.7 us)
Async XLA Ops:
  1.4 96.9 %collective-permute-start = (f32[1,8,128]{2,1,0:T(8,128)S(1)}, f32[1,8,128]{2,1,0:T(8,128)S(1)}, u32[]{:S(2)}, u32[]{:S(2)}) collective-permute-start(f32[1,8,128]{2,1,0:T(8,128)S(1)} %get-tuple-element.257), channel_id=1, source_target_pairs={{0,8},{8,16},{16,24},{24,32},{32,40},{40,48},{48,56},{56,64},{64,7... | collective-permute-start | bytes 12296 | tf_op jit(solution)/shard_map/ppermute | solution.py:25
  5.4 93.0 %collective-permute-start.1 = (f32[1,8,128]{2,1,0:T(8,128)S(1)}, f32[1,8,128]{2,1,0:T(8,128)S(1)}, u32[]{:S(2)}, u32[]{:S(2)}) collective-permute-start(f32[1,8,128]{2,1,0:T(8,128)S(1)} %get-tuple-element.256), channel_id=1, source_target_pairs={{8,0},{16,8},{24,16},{32,24},{40,32},{48,40},{56,48},{64,56},{72,6... | collective-permute-start | bytes 12296 | tf_op jit(solution)/shard_map/ppermute | solution.py:28
  16.2 76.4 %collective-permute-start.11 = (f32[4,1,64]{2,1,0:T(1,128)S(1)}, f32[4,1,64]{2,1,0:T(1,128)S(1)}, u32[]{:S(2)}, u32[]{:S(2)}) collective-permute-start(f32[4,1,64]{2,1,0:T(1,128)S(1)} %get-tuple-element.264), channel_id=1, source_target_pairs={{1,0},{2,1},{3,2},{4,3},{5,4},{6,5},{7,6},{9,8},{10,9},{11,10},{12... | collective-permute-start | bytes 3080 | tf_op jit(solution)/shard_map/ppermute | solution.py:28
  20.8 71.8 %collective-permute-start.10 = (f32[4,1,64]{2,1,0:T(1,128)S(1)}, f32[4,1,64]{2,1,0:T(1,128)S(1)}, u32[]{:S(2)}, u32[]{:S(2)}) collective-permute-start(f32[4,1,64]{2,1,0:T(1,128)S(1)} %get-tuple-element.263), channel_id=1, source_target_pairs={{0,1},{1,2},{2,3},{3,4},{4,5},{5,6},{6,7},{8,9},{9,10},{10,11},{11... | collective-permute-start | bytes 3080 | tf_op jit(solution)/shard_map/ppermute | solution.py:25
  93.0 11.7 %collective-permute-start.21 = (f32[1,2,32]{2,1,0:T(2,128)S(1)}, f32[1,2,32]{2,1,0:T(2,128)S(1)}, u32[]{:S(2)}, u32[]{:S(2)}) collective-permute-start(f32[1,2,32]{2,1,0:T(2,128)S(1)} %multiply_bitcast_fusion), channel_id=1, source_target_pairs={{8,0},{16,8},{24,16},{32,24},{40,32},{48,40},{56,48},{64,56},{72,6... | collective-permute-start | bytes 776 | tf_op jit(solution)/shard_map/ppermute | solution.py:28
  94.3 10.5 %collective-permute-start.20 = (f32[1,2,32]{2,1,0:T(2,128)S(1)}, f32[1,2,32]{2,1,0:T(2,128)S(1)}, u32[]{:S(2)}, u32[]{:S(2)}) collective-permute-start(f32[1,2,32]{2,1,0:T(2,128)S(1)} %multiply_bitcast_fusion), channel_id=1, source_target_pairs={{0,8},{8,16},{16,24},{24,32},{32,40},{40,48},{48,56},{56,64},{64,7... | collective-permute-start | bytes 776 | tf_op jit(solution)/shard_map/ppermute | solution.py:25
  105.9 12.1 %collective-permute-start.5 = (f32[3,8,1,8,128]{4,1,3,2,0:T(8,128)S(1)}, f32[3,8,1,8,128]{4,1,3,2,0:T(8,128)S(1)}, u32[]{:S(2)}, u32[]{:S(2)}) collective-permute-start(f32[3,8,1,8,128]{4,1,3,2,0:T(8,128)S(1)} %get-tuple-element.118), channel_id=1, source_target_pairs={{8,0},{16,8},{24,16},{32,24},{40,32},{48,40},{56,48},{64,56},{72,6... | collective-permute-start | bytes 294920 | tf_op jit(solution)/shard_map/ppermute | solution.py:28
  107.2 10.8 %collective-permute-start.4 = (f32[3,8,1,8,128]{4,1,3,2,0:T(8,128)S(1)}, f32[3,8,1,8,128]{4,1,3,2,0:T(8,128)S(1)}, u32[]{:S(2)}, u32[]{:S(2)}) collective-permute-start(f32[3,8,1,8,128]{4,1,3,2,0:T(8,128)S(1)} %get-tuple-element.117), channel_id=1, source_target_pairs={{0,8},{8,16},{16,24},{24,32},{32,40},{40,48},{48,56},{56,64},{64,7... | collective-permute-start | bytes 294920 | tf_op jit(solution)/shard_map/ppermute | solution.py:25
  111.6 31.9 %collective-permute-start.23 = (f32[3,1,32]{2,1,0:T(1,128)S(1)}, f32[3,1,32]{2,1,0:T(1,128)S(1)}, u32[]{:S(2)}, u32[]{:S(2)}) collective-permute-start(f32[3,1,32]{2,1,0:T(1,128)S(1)} %get-tuple-element.277), channel_id=1, source_target_pairs={{1,0},{2,1},{3,2},{4,3},{5,4},{6,5},{7,6},{9,8},{10,9},{11,10},{12... | collective-permute-start | bytes 1160 | tf_op jit(solution)/shard_map/ppermute | solution.py:28
  113.5 21.0 %collective-permute-start.22 = (f32[3,1,32]{2,1,0:T(1,128)S(1)}, f32[3,1,32]{2,1,0:T(1,128)S(1)}, u32[]{:S(2)}, u32[]{:S(2)}) collective-permute-start(f32[3,1,32]{2,1,0:T(1,128)S(1)} %get-tuple-element.276), channel_id=1, source_target_pairs={{0,1},{1,2},{2,3},{3,4},{4,5},{5,6},{6,7},{8,9},{9,10},{10,11},{11... | collective-permute-start | bytes 1160 | tf_op jit(solution)/shard_map/ppermute | solution.py:25
  126.4 8.1 %collective-permute-start.13 = (f32[3,8,1,8,128]{4,1,3,2,0:T(8,128)S(1)}, f32[3,8,1,8,128]{4,1,3,2,0:T(8,128)S(1)}, u32[]{:S(2)}, u32[]{:S(2)}) collective-permute-start(f32[3,8,1,8,128]{4,1,3,2,0:T(8,128)S(1)} %get-tuple-element.116), channel_id=1, source_target_pairs={{8,0},{16,8},{24,16},{32,24},{40,32},{48,40},{56,48},{64,56},{72,6... | collective-permute-start | bytes 294920 | tf_op jit(solution)/shard_map/ppermute | solution.py:28
  127.7 8.4 %collective-permute-start.12 = (f32[3,8,1,8,128]{4,1,3,2,0:T(8,128)S(1)}, f32[3,8,1,8,128]{4,1,3,2,0:T(8,128)S(1)}, u32[]{:S(2)}, u32[]{:S(2)}) collective-permute-start(f32[3,8,1,8,128]{4,1,3,2,0:T(8,128)S(1)} %get-tuple-element.115), channel_id=1, source_target_pairs={{0,8},{8,16},{16,24},{24,32},{32,40},{40,48},{48,56},{56,64},{64,7... | collective-permute-start | bytes 294920 | tf_op jit(solution)/shard_map/ppermute | solution.py:25
  136.1 7.5 collective-permute-start.15
  157.2 7.5 collective-permute-start.17
  158.5 7.3 collective-permute-start.16
  165.8 7.3 collective-permute-start.19
  174.5 7.7 collective-permute-start.25
  175.8 7.5 collective-permute-start.24
  183.4 7.0 collective-permute-start.27
  192.7 7.6 collective-permute-start.29
  194.0 7.2 collective-permute-start.28
  201.2 7.0 collective-permute-start.31
  210.1 8.1 %collective-permute-start.33 = (f32[3,8,1,4,64]{4,1,3,2,0:T(8,128)S(1)}, f32[3,8,1,4,64]{4,1,3,2,0:T(8,128)S(1)}, u32[]{:S(2)}, u32[]{:S(2)}) collective-permute-start(f32[3,8,1,4,64]{4,1,3,2,0:T(8,128)S(1)} %get-tuple-element.207), channel_id=1, source_target_pairs={{8,0},{16,8},{24,16},{32,24},{40,32},{48,40},{56,48},{64,56},{72,6... | collective-permute-start | bytes 73736 | tf_op jit(solution)/shard_map/ppermute | solution.py:28
  211.4 7.9 collective-permute-start.32
  228.0 8.0 collective-permute-start.37
  229.3 7.9 collective-permute-start.36
  256.3 8.1 %collective-permute-start.41 = (f32[3,8,1,8,128]{4,1,3,2,0:T(8,128)S(1)}, f32[3,8,1,8,128]{4,1,3,2,0:T(8,128)S(1)}, u32[]{:S(2)}, u32[]{:S(2)}) collective-permute-start(f32[3,8,1,8,128]{4,1,3,2,0:T(8,128)S(1)} %get-tuple-element.114), channel_id=1, source_target_pairs={{8,0},{16,8},{24,16},{32,24},{40,32},{48,40},{56,48},{64,56},{72,6... | collective-permute-start | bytes 294920 | tf_op jit(solution)/shard_map/ppermute | solution.py:28
  257.6 8.3 %collective-permute-start.40 = (f32[3,8,1,8,128]{4,1,3,2,0:T(8,128)S(1)}, f32[3,8,1,8,128]{4,1,3,2,0:T(8,128)S(1)}, u32[]{:S(2)}, u32[]{:S(2)}) collective-permute-start(f32[3,8,1,8,128]{4,1,3,2,0:T(8,128)S(1)} %get-tuple-element.113), channel_id=1, source_target_pairs={{0,8},{8,16},{16,24},{24,32},{32,40},{40,48},{48,56},{56,64},{64,7... | collective-permute-start | bytes 294920 | tf_op jit(solution)/shard_map/ppermute | solution.py:25
  266.0 7.2 collective-permute-start.43
  275.9 8.0 collective-permute-start.45
  277.2 8.3 %collective-permute-start.44 = (f32[3,8,1,8,128]{4,1,3,2,0:T(8,128)S(1)}, f32[3,8,1,8,128]{4,1,3,2,0:T(8,128)S(1)}, u32[]{:S(2)}, u32[]{:S(2)}) collective-permute-start(f32[3,8,1,8,128]{4,1,3,2,0:T(8,128)S(1)} %get-tuple-element.111), channel_id=1, source_target_pairs={{0,8},{8,16},{16,24},{24,32},{32,40},{40,48},{48,56},{56,64},{64,7... | collective-permute-start | bytes 294920 | tf_op jit(solution)/shard_map/ppermute | solution.py:25
  285.5 7.2 collective-permute-start.47
  295.4 8.1 %collective-permute-start.49 = (f32[3,8,1,8,128]{4,1,3,2,0:T(8,128)S(1)}, f32[3,8,1,8,128]{4,1,3,2,0:T(8,128)S(1)}, u32[]{:S(2)}, u32[]{:S(2)}) collective-permute-start(f32[3,8,1,8,128]{4,1,3,2,0:T(8,128)S(1)} %get-tuple-element.110), channel_id=1, source_target_pairs={{8,0},{16,8},{24,16},{32,24},{40,32},{48,40},{56,48},{64,56},{72,6... | collective-permute-start | bytes 294920 | tf_op jit(solution)/shard_map/ppermute | solution.py:28
  296.7 8.3 %collective-permute-start.48 = (f32[3,8,1,8,128]{4,1,3,2,0:T(8,128)S(1)}, f32[3,8,1,8,128]{4,1,3,2,0:T(8,128)S(1)}, u32[]{:S(2)}, u32[]{:S(2)}) collective-permute-start(f32[3,8,1,8,128]{4,1,3,2,0:T(8,128)S(1)} %get-tuple-element.109), channel_id=1, source_target_pairs={{0,8},{8,16},{16,24},{24,32},{32,40},{40,48},{48,56},{56,64},{64,7... | collective-permute-start | bytes 294920 | tf_op jit(solution)/shard_map/ppermute | solution.py:25
  305.1 8.0 collective-permute-start.51
  441.2 7.2 collective-permute-start.57
  476.7 7.1 collective-permute-start.63
  517.7 8.1 %collective-permute-start.73 = (f32[3,8,1,4,64]{4,1,3,2,0:T(8,128)S(1)}, f32[3,8,1,4,64]{4,1,3,2,0:T(8,128)S(1)}, u32[]{:S(2)}, u32[]{:S(2)}) collective-permute-start(f32[3,8,1,4,64]{4,1,3,2,0:T(8,128)S(1)} %get-tuple-element.199), channel_id=1, source_target_pairs={{8,0},{16,8},{24,16},{32,24},{40,32},{48,40},{56,48},{64,56},{72,6... | collective-permute-start | bytes 73736 | tf_op jit(solution)/shard_map/ppermute | solution.py:28
  519.0 7.9 collective-permute-start.72
  526.9 7.2 collective-permute-start.75
  535.6 8.0 collective-permute-start.77
  536.9 7.9 collective-permute-start.76
  563.9 8.7 %collective-permute-start.81 = (f32[3,8,1,8,128]{4,1,3,2,0:T(8,128)S(1)}, f32[3,8,1,8,128]{4,1,3,2,0:T(8,128)S(1)}, u32[]{:S(2)}, u32[]{:S(2)}) collective-permute-start(f32[3,8,1,8,128]{4,1,3,2,0:T(8,128)S(1)} %get-tuple-element.104), channel_id=1, source_target_pairs={{8,0},{16,8},{24,16},{32,24},{40,32},{48,40},{56,48},{64,56},{72,6... | collective-permute-start | bytes 294920 | tf_op jit(solution)/shard_map/ppermute | solution.py:28
  565.2 8.3 %collective-permute-start.80 = (f32[3,8,1,8,128]{4,1,3,2,0:T(8,128)S(1)}, f32[3,8,1,8,128]{4,1,3,2,0:T(8,128)S(1)}, u32[]{:S(2)}, u32[]{:S(2)}) collective-permute-start(f32[3,8,1,8,128]{4,1,3,2,0:T(8,128)S(1)} %get-tuple-element.103), channel_id=1, source_target_pairs={{0,8},{8,16},{16,24},{24,32},{32,40},{40,48},{48,56},{56,64},{64,7... | collective-permute-start | bytes 294920 | tf_op jit(solution)/shard_map/ppermute | solution.py:25
  573.6 7.1 collective-permute-start.83
  583.4 8.6 %collective-permute-start.85 = (f32[3,8,1,8,128]{4,1,3,2,0:T(8,128)S(1)}, f32[3,8,1,8,128]{4,1,3,2,0:T(8,128)S(1)}, u32[]{:S(2)}, u32[]{:S(2)}) collective-permute-start(f32[3,8,1,8,128]{4,1,3,2,0:T(8,128)S(1)} %get-tuple-element.102), channel_id=1, source_target_pairs={{8,0},{16,8},{24,16},{32,24},{40,32},{48,40},{56,48},{64,56},{72,6... | collective-permute-start | bytes 294920 | tf_op jit(solution)/shard_map/ppermute | solution.py:28
  584.7 8.3 %collective-permute-start.84 = (f32[3,8,1,8,128]{4,1,3,2,0:T(8,128)S(1)}, f32[3,8,1,8,128]{4,1,3,2,0:T(8,128)S(1)}, u32[]{:S(2)}, u32[]{:S(2)}) collective-permute-start(f32[3,8,1,8,128]{4,1,3,2,0:T(8,128)S(1)} %get-tuple-element.101), channel_id=1, source_target_pairs={{0,8},{8,16},{16,24},{24,32},{32,40},{40,48},{48,56},{56,64},{64,7... | collective-permute-start | bytes 294920 | tf_op jit(solution)/shard_map/ppermute | solution.py:25
  593.0 8.4 %collective-permute-start.87 = (f32[3,8,6,1,128]{4,1,3,2,0:T(8,128)S(1)}, f32[3,8,6,1,128]{4,1,3,2,0:T(8,128)S(1)}, u32[]{:S(2)}, u32[]{:S(2)}) collective-permute-start(f32[3,8,6,1,128]{4,1,3,2,0:T(8,128)S(1)} %get-tuple-element.82), channel_id=1, source_target_pairs={{1,0},{2,1},{3,2},{4,3},{5,4},{6,5},{7,6},{9,8},{10,9},{11,10},{12... | collective-permute-start | bytes 221192 | tf_op jit(solution)/shard_map/ppermute | solution.py:28
  (49 other events, 354.8 us)
where the time goes:
time: 818 us; the launch traced here: 805 us
  starting transfers between devices  316 us (39%)
  blocking collectives  284 us (35%)
  other arithmetic  90.7 us (11%)
  local copies, waits for them, and re-layouts  53.5 us (7%)
  waiting for transfers between devices  50.3 us (6%)
    ppermute x46, starting transfers between devices, padded_2(): lax.ppermute(lax.slice_in_dim(block, block.shape[dim] - width, None, axis...  235 us
    psum x2, blocking collectives, residual_gram(): return lax.psum(gram_matrix(residual, precond), ('gx', 'gy'))  204 us
    ppermute x46, starting transfers between devices, padded_2(): lax.ppermute(lax.slice_in_dim(block, 0, width, axis=dim), axis, backward)  81.8 us
    psum x1, blocking collectives, on_device(): pq_gram = lax.psum(gram_matrix(search, image), ('gx', 'gy'))  80.1 us
    scatter-add x1, other arithmetic, on_device(): flat = flat.at[:, case_ids, local_node].add(load_forces, mode='drop')  49.7 us
    ppermute x46, waiting for transfers between devices, padded_2(): lax.ppermute(lax.slice_in_dim(block, block.shape[dim] - width, None, axis...  45.2 us
  transfers between devices with their start and end apart: 92, of which 52 were waited for; matrix products, arithmetic and copies ran while one was open for 9% of the time, Pallas kernels for 0%

commit v1 on v0

v1 whole, which is shorter than its diff:
```python
import functools
import math

import jax
import jax.numpy as jnp
from jax import lax
from jax.experimental import pallas as pl
from jax.experimental.pallas import tpu as pltpu
from jax.sharding import PartitionSpec as P

CLASSES = 16
MU = 1.0 / 2.6
LAM = 0.3 / 0.52
MIN_MODULUS = 0.05
STEP_A = 1.0 / (2.7 + 2.1 * math.cos(math.pi / 4.0))
STEP_B = 1.0 / (2.7 - 2.1 * math.cos(math.pi / 4.0))
MESH = pl.DeviceIdType.MESH
F32 = jnp.float32

NX, NY, NC, NZ, LOADS = 4, 8, 8, 128, 64
H = 3
AX, AY = NX + 2 * H, NY + 2 * H
N8 = [(1, 0), (-1, 0), (0, 1), (0, -1), (1, 1), (1, -1), (-1, 1), (-1, -1)]
N14 = [(dx, dy) for dx in (1, -1, 2, -2, 0) for dy in (0, 1, -1) if (dx, dy) != (0, 0)]

K_E, K_F, K_E2, K_G, K_X2, K_G2, K_X2C, K_G3, K_EC = 0, 1, 2, 3, 5, 7, 9, 11, 13
KINDS = 15


def lanes():
    return lax.broadcasted_iota(jnp.int32, (NC, NZ), 1)


def subl():
    return lax.broadcasted_iota(jnp.int32, (NC, NZ), 0)


def up(v, s):
    return pltpu.roll(v, NZ - s, 1)


def down(v, s):
    return pltpu.roll(v, s, 1)


def pair_sum(v, s):
    other = jnp.where((lanes() & s) == 0, up(v, s), down(v, s))
    return v + other


def row(v):
    return jnp.broadcast_to(v, (NC, NZ))


def span(d, n, h, base):
    if d > 0:
        return n - h, base - h, h
    if d < 0:
        return 0, base + n, h
    return 0, base, n


def coefficients(s, e_at, f_at, low, mid, inv, co):
    kx, ky, kzp, kzm, dm, cw, cf, ff, ad, bd = co
    last = lanes() >= NZ - s
    first = lanes() < s
    half = 0.5 * MU

    def lower(i, carry):
        for j in range(*low[1]):
            e, f = e_at(i, j), f_at(i, j)
            fx, fy = f_at(i + 1, j), f_at(i, j + 1)
            fzp = jnp.where(last, 0.0, up(f, s))
            fzm = jnp.where(first, 0.0, down(f, s))
            ezp, ezm = up(e, s), down(e, s)
            kx[i, j] = half * (e + e_at(i + 1, j)) * f * fx
            ky[i, j] = half * (e + e_at(i, j + 1)) * f * fy
            kzp[i, j] = half * (e + ezp) * f * fzp
            kzm[i, j] = half * (ezm + e) * f * fzm
            le = LAM * e
            cw[0, i, j] = le * fx
            cw[1, i, j] = le * fy
            cw[2, i, j] = le * fzp
            cf[i, j] = le * f
            ff[i, j] = f
        return carry

    lax.fori_loop(low[0][0], low[0][1], lower, 0)

    def total(i, j):
        e = e_at(i, j)
        ezp = jnp.where(last, 0.0, up(e, s))
        ezm = jnp.where(first, 0.0, down(e, s))
        ex, ey = e_at(i - 1, j), e_at(i, j - 1)
        d = half * (ex + e_at(i + 1, j) + ey + e_at(i, j + 1) + ezm + ezp + 6.0 * e)
        return e, (ex, ey, ezm), d

    def middle(i, carry):
        for j in range(*mid[1]):
            f = f_at(i, j)
            _, _, d = total(i, j)
            dm[i, j] = f * d + (1.0 - f)
        return carry

    lax.fori_loop(mid[0][0], mid[0][1], middle, 0)

    def smoother(i, carry):
        for j in range(*inv[1]):
            f = f_at(i, j)
            e, below, d = total(i, j)
            for c in range(3):
                diag = jnp.where(e > 0.0, d + LAM * (e + below[c]), 1.0)
                dinv = jnp.where(e > 0.0, f / diag + (1.0 - f), 0.0)
                ad[c, i, j] = STEP_A * dinv
                bd[c, i, j] = STEP_B * dinv
        return carry

    lax.fori_loop(inv[0][0], inv[0][1], smoother, 0)


def divergence(v, s, xr, yr, co, w):
    cw, cf = co[5], co[6]

    def body(i, carry):
        for j in range(yr[0] - 1, yr[1]):
            a, b, c = v[0, i, j], v[1, i, j], v[2, i, j]
            w[i, j] = (
                cw[0, i, j] * v[0, i + 1, j]
                + cw[1, i, j] * v[1, i, j + 1]
                + cw[2, i, j] * up(c, s)
                - cf[i, j] * (a + b + c)
            )
        return carry

    lax.fori_loop(xr[0] - 1, xr[1], body, 0)


def plane(v, s, i, j, co, w, wmask):
    kx, ky, kzp, kzm, dm, _, _, ff = co[:8]
    wc = w[i, j]
    wz = jnp.where(wmask, 0.0, down(wc, s))
    below = (w[i - 1, j], w[i, j - 1], wz)
    f = ff[i, j]
    k = (kx[i, j], kx[i - 1, j], ky[i, j], ky[i, j - 1], kzp[i, j], kzm[i, j])
    out = []
    for c in range(3):
        vc = v[c, i, j]
        lap = dm[i, j] * vc
        lap -= k[0] * v[c, i + 1, j] + k[1] * v[c, i - 1, j]
        lap -= k[2] * v[c, i, j + 1] + k[3] * v[c, i, j - 1]
        lap -= k[4] * up(vc, s) + k[5] * down(vc, s)
        out.append((vc, lap + f * (below[c] - wc)))
    return out


def apply(v, s, xr, yr, co, w, emit):
    divergence(v, s, xr, yr, co, w)
    wmask = lanes() < s

    def body(i, carry):
        for j in range(*yr):
            for c, (vc, av) in enumerate(plane(v, s, i, j, co, w, wmask)):
                emit(c, i, j, vc, av)
        return carry

    lax.fori_loop(xr[0], xr[1], body, 0)


def smooth(v, s, xr, yr, co, w, rhs, step, out):
    def emit(c, i, j, vc, av):
        out[c, i, j] = vc + step[c, i, j] * (rhs[c, i, j] - av)

    apply(v, s, xr, yr, co, w, emit)


def restrict(v, s, xr, yr, co, w, rhs, coarse):
    divergence(v, s, xr, yr, co, w)
    wmask = lanes() < s

    def body(q, carry):
        for y2 in range((yr[1] - yr[0]) // 2):
            acc = [None] * 3
            for a in range(2):
                for b in range(2):
                    i, j = xr[0] + 2 * q + a, yr[0] + 2 * y2 + b
                    for c, (_, av) in enumerate(plane(v, s, i, j, co, w, wmask)):
                        rem = rhs[c, i, j] - av
                        acc[c] = rem if acc[c] is None else acc[c] + rem
            for c in range(3):
                coarse[c, q, y2] = pair_sum(acc[c], s)
        return carry

    lax.fori_loop(0, (xr[1] - xr[0]) // 2, body, 0)


def column(m, i):
    picked = jnp.where(lanes() == subl(), row(m[i : i + 1, :]), 0.0)
    return row(jnp.sum(picked, axis=1, keepdims=True))


def mm(a, b):
    return sum(row(a[:, k : k + 1]) * row(b[k : k + 1, :]) for k in range(NC))


def mtm(a, b):
    return sum(column(a, k) * row(b[k : k + 1, :]) for k in range(NC))


def solve(matrix, rhs):
    aug = jnp.where(lanes() < NC, matrix, pltpu.roll(rhs, NC, 1))
    for k in range(NC):
        scaled = row(aug[k : k + 1, :]) / row(aug[k : k + 1, k : k + 1])
        aug = jnp.where(subl() == k, scaled, aug - row(aug[:, k : k + 1]) * scaled)
    return up(aug, NC)


def kernel(
    size_x, size_y,
    src, dens, mask, nodes, forces, xo, ro,
    eb, fb, e2b, ex, fx, e2x, e3x, one,
    g, pv, a1, a2, a3, a4, xb, w, loadbuf,
    kx, ky, kzp, kzm, dm, cw, cf, ff, ad, bd,
    kx2, ky2, kzp2, kzm2, dm2, cw2, cf2, ff2, ad2, bd2,
    kx3, ky3, kzp3, kzm3, dm3, cw3, cf3, ff3, ad3, bd3,
    t2, g2r, x2r, ecr, g2u, b1, b2, b3, b4, w2, e2u,
    t3, g3r, g3u, c1, c2, w3,
    gram, ps1, ps2, mats, raw,
    send, recv, psend, precv,
):
    gx, gy = lax.axis_index("gx"), lax.axis_index("gy")
    co1 = (kx, ky, kzp, kzm, dm, cw, cf, ff, ad, bd)
    co2 = (kx2, ky2, kzp2, kzm2, dm2, cw2, cf2, ff2, ad2, bd2)
    co3 = (kx3, ky3, kzp3, kzm3, dm3, cw3, cf3, ff3, ad3, bd3)
    even = (lanes() & 1) == 0
    low2 = (lanes() & 2) == 0

    def valid(dx, dy):
        return (gx + dx >= 0) & (gx + dx < size_x) & (gy + dy >= 0) & (gy + dy < size_y)

    def message(kind, k, d, refs):
        a, b = refs(*d)
        return pltpu.make_async_remote_copy(
            src_ref=a, dst_ref=b, send_sem=send.at[kind, k], recv_sem=recv.at[kind, k],
            device_id=(gx + d[0], gy + d[1]), device_id_type=MESH,
        )

    def start(kind, group, refs):
        for k, d in enumerate(group):
            @pl.when(valid(*d))
            def _():
                message(kind, k, d, refs).start()

    def arrive(kind, group, refs):
        for k, d in enumerate(group):
            @pl.when(valid(-d[0], -d[1]))
            def _():
                message(kind, k, d, refs).wait_recv()

    def sent(kind, group, refs):
        for k, d in enumerate(group):
            @pl.when(valid(*d))
            def _():
                message(kind, k, d, refs).wait_send()

    def boxes(ref):
        return lambda dx, dy: (ref.at[1, 1], ref.at[1 - dx, 1 - dy])

    def e2_refs(dx, dy):
        return e2b.at[2, 1], e2b.at[2 - dx, 1 - dy]

    def halo(source, target, h):
        def refs(dx, dy):
            sx, tx, nx = span(dx, NX, h, H)
            sy, ty, ny = span(dy, NY, h, H)
            a = source.at[:, pl.ds(H + sx, nx), pl.ds(H + sy, ny)]
            return a, target.at[:, pl.ds(tx, nx), pl.ds(ty, ny)]
        return refs

    def coarse_refs(ref):
        def refs(dx, dy):
            sy, ty, ny = span(dy, 4, 2, 2)
            return ref.at[:, 1, pl.ds(2 + sy, ny)], ref.at[:, 1 - dx, pl.ds(ty, ny)]
        return refs

    def g3_refs(ref):
        return lambda dx, dy: (ref.at[:, 2, 1], ref.at[:, 2 - dx, 1 - dy])

    zero3 = jnp.zeros((NX, NY, NZ), F32)
    for bx in range(3):
        for by in range(3):
            eb[bx, by] = zero3
            fb[bx, by] = zero3
    for bx in range(5):
        for by in range(3):
            e2b[bx, by] = jnp.zeros((NC, NZ), F32)
    for x in range(NX):
        rel = (dens[x].astype(F32) + 1.0) / CLASSES
        eb[1, 1, x] = MIN_MODULUS + (1.0 - MIN_MODULUS) * rel * rel * rel
        fb[1, 1, x] = 1.0 - mask[x].astype(F32)
    halves = []
    for q in range(2):
        t = eb[1, 1, 2 * q] + eb[1, 1, 2 * q + 1]
        halves.append(0.25 * pair_sum(t + pltpu.roll(t, NY - 1, 0), 1))
    e2b[2, 1] = jnp.where((subl() & 1) == 0, halves[0], pltpu.roll(halves[1], 1, 0))

    for c in range(3):
        for x in range(NX):
            for y in range(NY):
                raw[c, H + x, H + y] = src[pl.ds((c * NC * NX + x) * NY + y, NC, stride=NX * NY), :]

    bar = pltpu.get_barrier_semaphore()
    corners = [(dx, dy) for dx in (1, -1, 2, -2) for dy in (1, -1)]
    peers = jnp.int32(size_x + size_y - 2)

    def greet_x(d, carry):
        pl.semaphore_signal(bar, inc=1, device_id=(lax.rem(gx + d, size_x), gy), device_id_type=MESH)
        return carry

    def greet_y(d, carry):
        pl.semaphore_signal(bar, inc=1, device_id=(gx, lax.rem(gy + d, size_y)), device_id_type=MESH)
        return carry

    lax.fori_loop(1, size_x, greet_x, 0)
    lax.fori_loop(1, size_y, greet_y, 0)
    for d in corners:
        peers = peers + jnp.where(valid(*d), 1, 0)

        @pl.when(valid(*d))
        def _():
            pl.semaphore_signal(bar, inc=1, device_id=(gx + d[0], gy + d[1]), device_id_type=MESH)
    pl.semaphore_wait(bar, peers)

    start(K_E, N8, boxes(eb))
    start(K_F, N8, boxes(fb))
    start(K_G, N8, halo(raw, raw, 2))
    start(K_E2, N14, e2_refs)

    def load_case(i, carry):
        node = nodes[pl.ds(i, 1), :]
        nz = lax.rem(node, NZ)
        nyx = lax.div(node, NZ)
        ny = lax.rem(nyx, size_y * NY) - gy * NY + 2
        nx = lax.div(nyx, size_y * NY) - gx * NX + 2
        hot = jnp.where(lax.broadcasted_iota(jnp.int32, (NZ, LOADS), 0) == nz, 1.0, 0.0)
        rows = lax.broadcasted_iota(jnp.int32, (16, LOADS), 0)
        parts = []
        for c in range(3):
            force = forces[c, pl.ds(i, 1), :]
            for x in range(8):
                parts.append(jnp.where((rows == ny) & (nx == x), force, 0.0))
        got = lax.dot_general(
            jnp.concatenate(parts, axis=0), hot, (((1,), (1,)), ((), ())),
            precision=lax.Precision.HIGHEST, preferred_element_type=F32,
        )
        for k in range(24):
            loadbuf[pl.ds(k * 96 + i, 8, stride=NC), :] = got[16 * k : 16 * k + 8]
            loadbuf[pl.ds(k * 96 + 64 + i, 4, stride=NC), :] = got[16 * k + 8 : 16 * k + 12]
        return carry

    lax.fori_loop(0, NC, load_case, 0)

    arrive(K_E, N8, boxes(eb))
    arrive(K_F, N8, boxes(fb))
    for i in range(AX):
        for j in range(AY):
            bx, xl, by, yl = (i + 1) // 4, (i + 1) % 4, (j + 5) // 8, (j + 5) % 8
            ex[i, j] = row(eb[bx, by, xl, yl : yl + 1, :])
            fx[i, j] = row(fb[bx, by, xl, yl : yl + 1, :])
    coefficients(
        1, lambda i, j: ex[i, j], lambda i, j: fx[i, j],
        ((0, 9), (0, 13)), ((1, 9), (1, 13)), ((1, 9), (1, 13)), co1,
    )

    arrive(K_G, N8, halo(raw, raw, 2))

    def first_rhs(i, carry):
        for c in range(3):
            for j in range(1, 13):
                k = ((c * 8 + i - 1) * 12 + j - 1) * NC
                total = fx[i, j] * (raw[c, i, j] + loadbuf[pl.ds(pl.multiple_of(k, NC), NC), :])
                total = jnp.where(ex[i, j] > 0.0, total, 0.0)
                g[0, c, i, j] = total
        return carry

    lax.fori_loop(1, 9, first_rhs, 0)

    def unpack(p):
        return jnp.where(even, p, down(p, 1)), jnp.where(even, up(p, 1), p)

    def unpack_field(packed, out, add=None):
        for c in range(3):
            for bx in range(3):
                for j in range(8):
                    for a, val in enumerate(unpack(packed[c, bx, j])):
                        i = 2 * bx + a
                        val = jnp.where(ad2[0, i, j] > 0.0, val, 0.0)
                        if add is not None:
                            val = val + add[c, i // 2 + 1, j // 2 + 1]
                        out[c, i, j] = val

    def pack_field(field, base, packed):
        for c in range(3):
            for j in range(4):
                packed[c, 1, 2 + j] = jnp.where(even, field[c, base[0], base[1] + j], field[c, base[0] + 1, base[1] + j])

    def cycle(it, carry):
        rhs = g.at[it]
        own = ((H, H + NX), (H, H + NY))
        one_out = ((H - 1, H + NX + 1), (H - 1, H + NY + 1))
        two_out = ((H - 2, H + NX + 2), (H - 2, H + NY + 2))
        x_refs = halo(a2, xb.at[it], 3)
        g2, x2, ec, g3 = g2r.at[it], x2r.at[it], ecr.at[it], g3r.at[it]

        @pl.when(it == 1)
        def _():
            def clean(i, c2_):
                for c in range(3):
                    for j in range(1, 13):
                        rhs[c, i, j] = jnp.where(ex[i, j] > 0.0, rhs[c, i, j], 0.0)
                return c2_
            lax.fori_loop(1, 9, clean, 0)

        def first(i, c2_):
            for c in range(3):
                for j in range(1, 13):
                    a1[c, i, j] = ad[c, i, j] * rhs[c, i, j]
            return c2_

        lax.fori_loop(1, 9, first, 0)
        smooth(a1, 1, *one_out, co1, w, rhs, bd, a2)
        restrict(a2, 1, *own, co1, w, rhs, t2)
        pack_field(t2, (0, 0), g2)
        start(K_G2 + it, N8, coarse_refs(g2))
        start(K_X2 + it, N8, x_refs)

        @pl.when(it == 0)
        def _():
            arrive(K_E2, N14, e2_refs)
            for i in range(10):
                for j in range(12):
                    k = (j % 4) * 2 + i % 2
                    e2x[i, j] = row(e2b[i // 2, j // 4, k : k + 1, :])
            for i in range(5):
                for j in range(6):
                    t = e2x[2 * i, 2 * j] + e2x[2 * i + 1, 2 * j] + e2x[2 * i, 2 * j + 1] + e2x[2 * i + 1, 2 * j + 1]
                    e3x[i, j] = 0.25 * pair_sum(t, 2)
            one[...] = jnp.ones((NC, NZ), F32)
            coefficients(
                2, lambda i, j: e2x[i + 2, j + 2], lambda i, j: one[...],
                ((0, 5), (0, 7)), ((1, 5), (1, 7)), ((0, 6), (0, 8)), co2,
            )
            coefficients(
                4, lambda i, j: e3x[i, j], lambda i, j: one[...],
                ((0, 4), (0, 5)), ((1, 4), (1, 5)), ((1, 4), (1, 5)), co3,
            )

        arrive(K_G2 + it, N8, coarse_refs(g2))
        unpack_field(g2, g2u)
        for c in range(3):
            for i in range(6):
                for j in range(8):
                    b1[c, i, j] = ad2[c, i, j] * g2u[c, i, j]
        own2, out2 = ((2, 4), (2, 6)), ((1, 5), (1, 7))
        smooth(b1, 2, *out2, co2, w2, g2u, bd2, b2)
        pack_field(b2, (2, 2), x2)
        start(K_X2C + it, N8, coarse_refs(x2))
        restrict(b2, 2, *own2, co2, w2, g2u, t3)
        for c in range(3):
            r0, r1 = t3[c, 0, 0], t3[c, 0, 1]
            s0, s1 = ad3[c, 2, 2] * r0, ad3[c, 2, 3] * r1
            g3[c, 2, 1] = jnp.where(low2, jnp.where(even, r0, r1), jnp.where(even, s0, s1))
        start(K_G3 + it, N14, g3_refs(g3))
        arrive(K_G3 + it, N14, g3_refs(g3))
        for c in range(3):
            for bx in range(5):
                for by in range(3):
                    for a, q in enumerate(unpack(g3[c, bx, by])):
                        keep = e3x[bx, 2 * by + a] > 0.0
                        g3u[c, bx, 2 * by + a] = jnp.where(keep, jnp.where(low2, q, down(q, 2)), 0.0)
                        c1[c, bx, 2 * by + a] = jnp.where(keep, jnp.where(low2, up(q, 2), q), 0.0)
        smooth(c1, 4, (1, 4), (1, 5), co3, w3, g3u, bd3, c2)
        arrive(K_X2C + it, N8, coarse_refs(x2))
        unpack_field(x2, b3, add=c2)
        smooth(b3, 2, *out2, co2, w2, g2u, bd2, b4)
        smooth(b4, 2, *own2, co2, w2, g2u, ad2, b1)
        pack_field(b1, (2, 2), ec)
        start(K_EC + it, N8, coarse_refs(ec))
        arrive(K_EC + it, N8, coarse_refs(ec))
        unpack_field(ec, e2u)
        arrive(K_X2 + it, N8, x_refs)

        def correct(i, rows, from_own):
            for c in range(3):
                for j in range(AY):
                    inner = from_own and H <= j < H + NY
                    old = a2[c, i, j] if inner else xb[it, c, i, j]
                    keep = ex[i, j] > 0.0
                    e = e2u[c, (i + 1) // 2, (j + 1) // 2]
                    a3[c, i, j] = jnp.where(keep, old + fx[i, j] * e, 0.0)

        for i in range(AX):
            correct(i, None, H <= i < H + NX)
        smooth(a3, 1, *two_out, co1, w, rhs, bd, a4)
        smooth(a4, 1, *one_out, co1, w, rhs, ad, pv.at[it])

        def keep_image(c, i, j, vc, av):
            g[it + 1, c, i, j] = av

        apply(pv.at[it], 1, *own, co1, w, keep_image)

        q_refs = halo(g.at[1], g.at[1], 2)

        @pl.when(it == 0)
        def _():
            start(K_G + 1, N8, q_refs)

        def gram_plane(i, accs):
            accs = list(accs)
            for c in range(3):
                for j in range(H, H + NY):
                    left = [g[q, c, i, j] for q in range(2)] + [jnp.where(it == 1, g[2, c, i, j], 0.0)]
                    for k in range(NC):
                        right = row(pv[it, c, i, j, k : k + 1, :])
                        for q in range(3):
                            accs[q * NC + k] = accs[q * NC + k] + left[q] * right
            return tuple(accs)

        zeros = tuple(jnp.zeros((NC, NZ), F32) for _ in range(3 * NC))
        accs = lax.fori_loop(H, H + NX, gram_plane, zeros)
        out = jnp.zeros((NC, NZ), F32)
        for q in range(3):
            for k in range(NC):
                out = jnp.where(lanes() == q * NC + k, row(jnp.sum(accs[q * NC + k], axis=1, keepdims=True)), out)
        gram[it] = out

        @pl.when(it == 0)
        def _():
            arrive(K_G + 1, N8, q_refs)
            sent(K_G + 1, N8, q_refs)

        sent(K_X2 + it, N8, x_refs)
        sent(K_G2 + it, N8, coarse_refs(g2))
        sent(K_X2C + it, N8, coarse_refs(x2))
        sent(K_G3 + it, N14, g3_refs(g3))
        sent(K_EC + it, N8, coarse_refs(ec))
        return carry

    lax.fori_loop(0, 2, cycle, 0)
    sent(K_E, N8, boxes(eb))
    sent(K_F, N8, boxes(fb))
    sent(K_G, N8, halo(raw, raw, 2))
    sent(K_E2, N14, e2_refs)

    def total(buffer, me, count, place, base):
        def copy(d):
            return pltpu.make_async_remote_copy(
                src_ref=buffer.at[me], dst_ref=buffer.at[me],
                send_sem=psend.at[base + d], recv_sem=precv.at[base + me],
                device_id=place(lax.rem(me + d, count)), device_id_type=MESH,
            )

        def landing(d):
            other = lax.rem(me + d, count)
            return pltpu.make_async_remote_copy(
                src_ref=buffer.at[other], dst_ref=buffer.at[other],
                send_sem=psend.at[base + d], recv_sem=precv.at[base + other],
                device_id=place(other), device_id_type=MESH,
            )

        def go(d, carry):
            copy(d).start()
            return carry

        def take(d, carry):
            landing(d).wait_recv()
            return carry

        def done(d, carry):
            copy(d).wait_send()
            return carry

        lax.fori_loop(1, count, go, 0)
        lax.fori_loop(1, count, take, 0)
        lax.fori_loop(1, count, done, 0)
        out = buffer[0]
        for k in range(1, count):
            out = out + buffer[k]
        return out

    ps1[gy] = jnp.where(lanes() < 2 * NC, gram[0], pltpu.roll(gram[1], 2 * NC, 1))
    ps2[gx] = total(ps1, gy, size_y, lambda k: (gx, k), 0)
    sums = total(ps2, gx, size_x, lambda k: (k, gy), size_y)

    rz = sums
    qp = up(sums, NC)
    ru = up(sums, 2 * NC)
    qu = up(sums, 3 * NC)
    wu = up(sums, 4 * NC)
    eye = jnp.where(lanes() == subl(), 1.0, 0.0)
    alpha = solve(qp, rz)
    inverse = solve(rz, eye)
    rz2 = rz - mm(ru, alpha) + mtm(alpha, mm(qu, alpha) - qp)
    mix = eye + mm(inverse, rz2)
    quw = mm(qu, alpha)
    pq2 = mtm(mix, mtm(qp, mix) - quw) + mtm(alpha, mtm(wu, alpha) - mtm(qu, mix))
    alpha2 = solve(pq2, rz2)
    one_m = alpha + mm(mix, alpha2)
    two_m = mm(alpha, alpha2)
    for k in range(NC):
        mats[0, k] = column(one_m, k)
        mats[1, k] = column(two_m, k)

    def finish(x, carry):
        m1 = [mats[0, k] for k in range(NC)]
        m2 = [mats[1, k] for k in range(NC)]
        i = H + x
        for c in range(3):
            for y in range(NY):
                j = H + y
                sol = jnp.zeros((NC, NZ), F32)
                res = g[0, c, i, j]
                for k in range(NC):
                    sol = sol + row(pv[0, c, i, j, k : k + 1, :]) * m1[k]
                    sol = sol - row(pv[1, c, i, j, k : k + 1, :]) * m2[k]
                    res = res - row(g[1, c, i, j, k : k + 1, :]) * m1[k]
                    res = res + row(g[2, c, i, j, k : k + 1, :]) * m2[k]
                at = pl.ds((c * NC * NX + x) * NY + y, NC, stride=NX * NY)
                xo[at, :] = sol
                ro[at, :] = res
        return carry

    lax.fori_loop(0, NX, finish, 0)


def on_device(size_x, size_y, source_field, density_class, fixed_mask, load_nodes, load_forces):
    rows = 3 * NC * NX * NY
    tile = (NC, NZ)

    def vm(*dims):
        return pltpu.VMEM(dims + tile, F32)

    def level(nx, ny):
        return [vm(nx, ny)] * 5 + [vm(3, nx, ny), vm(nx, ny), vm(nx, ny), vm(3, nx, ny), vm(3, nx, ny)]

    scratch = [
        pltpu.VMEM((3, 3, NX, NY, NZ), F32), pltpu.VMEM((3, 3, NX, NY, NZ), F32), vm(5, 3),
        vm(AX, AY), vm(AX, AY), vm(10, 12), vm(5, 6), vm(),
        vm(3, 3, AX, AY), vm(2, 3, AX, AY), vm(3, AX, AY), vm(3, AX, AY), vm(3, AX, AY), vm(3, AX, AY),
        vm(2, 3, AX, AY), vm(AX, AY), pltpu.VMEM((3 * 8 * 12 * NC, NZ), F32),
    ]
    scratch += level(AX, AY) + level(6, 8) + level(5, 6)
    scratch += [vm(3, 2, 4), vm(2, 3, 3, 8), vm(2, 3, 3, 8), vm(2, 3, 3, 8)]
    scratch += [vm(3, 6, 8)] * 5 + [vm(6, 8), vm(3, 6, 8)]
    scratch += [vm(3, 1, 2), vm(2, 3, 5, 3), vm(3, 5, 6), vm(3, 5, 6), vm(3, 5, 6), vm(5, 6)]
    scratch += [vm(2), vm(size_y), vm(size_x), vm(2, NC), vm(3, AX, AY)]
    sems = pltpu.SemaphoreType.DMA
    scratch += [sems((KINDS, len(N14))), sems((KINDS, len(N14))), sems((size_x + size_y,)), sems((size_x + size_y,))]
    spec = pl.BlockSpec(memory_space=pltpu.VMEM)
    shape = jax.ShapeDtypeStruct((rows, NZ), F32)
    sol, res = pl.pallas_call(
        functools.partial(kernel, size_x, size_y),
        out_shape=(shape, shape),
        in_specs=[spec] * 5,
        out_specs=(spec, spec),
        scratch_shapes=scratch,
        compiler_params=pltpu.CompilerParams(
            collective_id=0, has_side_effects=True, vmem_limit_bytes=56 * 1024 * 1024
        ),
        name="block_pcg",
    )(source_field.reshape(rows, NZ), density_class, fixed_mask, load_nodes, load_forces)
    return sol.reshape(source_field.shape), res.reshape(source_field.shape)


def solution(mesh):
    placed = (P(None, None, "gx", "gy", None), P("gx", "gy", None), P("gx", "gy", None), P(), P())
    return jax.shard_map(
        functools.partial(on_device, mesh.shape["gx"], mesh.shape["gy"]),
        mesh=mesh,
        in_specs=placed,
        out_specs=(P(None, None, "gx", "gy", None), P(None, None, "gx", "gy", None)),
        check_vma=False,
    )
```

time: 818 us -> 137 us (0.17); the launches traced: 805 us -> 136 us
  starting transfers between devices: 316 us -> 0 us
  blocking collectives: 284 us -> 0 us
  Pallas kernels: 0 us -> 133 us
  other arithmetic: 90.7 us -> 0 us
  local copies, waits for them, and re-layouts: 53.5 us -> 2.57 us
  waiting for transfers between devices: 50.3 us -> 0 us
    ppermute x92 -> x0, starting transfers between devices: 316 us -> none  [the longest x46 235 us: padded_2(): lax.ppermute(lax.slice_in_dim(block, block.shape[dim] - width, None, axis...]
    psum x3 -> x0, blocking collectives: 284 us -> none  [the longest x2 204 us: residual_gram(): return lax.psum(gram_matrix(residual, precond), ('gx', 'gy'))]
    pallas_call x0 -> x1, Pallas kernels: none -> 133 us  [on_device(): pl.pallas_call(functools.partial(kernel, size_x, size_y), out_shape=(shap...]
    ppermute x92 -> x0, waiting for transfers between devices: 50.3 us -> none  [the longest x46 45.2 us: padded_2(): lax.ppermute(lax.slice_in_dim(block, block.shape[dim] - width, None, axis...]
    scatter-add x1 -> x0, other arithmetic: 49.7 us -> none  [on_device(): flat = flat.at[:, case_ids, local_node].add(load_forces, mode='drop')]
    reshape x4 -> x0, local copies, waits for them, and re-layouts: 19.7 us -> none  [the longest x1 10 us: on_device(): right = levels[0][1] * flat.reshape(source_field.shape)]
    reduce_sum x8 -> x0, other arithmetic: 14.6 us -> none  [restrict_sum(): return jnp.sum(shaped, axis=(-5, -3, -1))]
    broadcast_in_dim x8 -> x0, local copies, waits for them, and re-layouts: 12.2 us -> none  [prolong(): jnp.broadcast_to(expanded, lead + (extent[0], 2, extent[1], 2, extent[2],...]
  transfers between devices with their start and end apart: 92 -> 0, of which waited for: 52 -> 0; matrix products, arithmetic and copies ran while one was open for 9% -> 0% of each run, Pallas kernels for 0% -> 0%
where the time goes in v1:
time: 137 us; the launch traced here: 136 us
  Pallas kernels  133 us (97%)
  local copies, waits for them, and re-layouts  2.57 us (2%)
    pallas_call x1, Pallas kernels, on_device(): pl.pallas_call(functools.partial(kernel, size_x, size_y), out_shape=(shap...  133 us

profile of v1, /device:TPU:1, one launch (start us, length us, event | category | flops | bytes accessed | tf_op | source)
XLA Modules:
  0.0 136.4 jit_solution(976278655200192437)
XLA Ops:
  0.6 133.2 %block_pcg.1 = (f32[768,128]{1,0:T(8,128)}, f32[768,128]{1,0:T(8,128)}) custom-call(f32[768,128]{1,0:T(8,128)} %bitcast.3, s32[4,8,128]{2,1,0:T(8,128)} %dens.1, s32[4,8,128]{2,1,0:T(8,128)} %mask.1, s32[8,64]{1,0:T(8,128)} %nodes.1, f32[3,8,64]{2,1,0:T(8,128)} %forces.1), custom_call_target="tpu_custom_call" | custom-call | tf_op jit(solution)/shard_map/block_pcg/pallas_call | solution.py:660
  133.8 0.0 copy-start
  133.8 1.8 %copy.9 = f32[3,8,4,8,128]{4,3,2,1,0:T(8,128)} copy(f32[3,8,4,8,128]{4,3,2,1,0:T(8,128)} %bitcast.5) | data formatting | bytes 786432
  135.6 0.0 copy-done
  135.6 0.7 copy.10
Async XLA Ops:
  133.8 1.8 %copy-start = (f32[768,128]{1,0:T(8,128)S(1)}, f32[768,128]{1,0:T(8,128)}, u32[]{:S(2)}) copy-start(f32[768,128]{1,0:T(8,128)} %get-tuple-element.5) | copy-start | bytes 1179652

commit v2 on v1

--- a/solution.py
+++ b/solution.py
@@ -60,142 +60,167 @@
     return 0, base, n
 
 
-def coefficients(s, e_at, f_at, low, mid, inv, co):
+def coefficients(s, e_at, f_at, low, inv, co, unroll=False):
     kx, ky, kzp, kzm, dm, cw, cf, ff, ad, bd = co
     last = lanes() >= NZ - s
     first = lanes() < s
     half = 0.5 * MU
 
     def lower(i, carry):
+        pending = []
         for j in range(*low[1]):
             e, f = e_at(i, j), f_at(i, j)
             fx, fy = f_at(i + 1, j), f_at(i, j + 1)
             fzp = jnp.where(last, 0.0, up(f, s))
             fzm = jnp.where(first, 0.0, down(f, s))
             ezp, ezm = up(e, s), down(e, s)
-            kx[i, j] = half * (e + e_at(i + 1, j)) * f * fx
-            ky[i, j] = half * (e + e_at(i, j + 1)) * f * fy
-            kzp[i, j] = half * (e + ezp) * f * fzp
-            kzm[i, j] = half * (ezm + e) * f * fzm
             le = LAM * e
-            cw[0, i, j] = le * fx
-            cw[1, i, j] = le * fy
-            cw[2, i, j] = le * fzp
-            cf[i, j] = le * f
-            ff[i, j] = f
+            hf = half * f
+            pending += [
+                (kx, (i, j), (e + e_at(i + 1, j)) * (hf * fx)),
+                (ky, (i, j), (e + e_at(i, j + 1)) * (hf * fy)),
+                (kzp, (i, j), (e + ezp) * (hf * fzp)),
+                (kzm, (i, j), (ezm + e) * (hf * fzm)),
+                (cw, (0, i, j), le * fx),
+                (cw, (1, i, j), le * fy),
+                (cw, (2, i, j), le * fzp),
+                (cf, (i, j), le * f),
+                (ff, (i, j), f),
+            ]
+            if j % 3 == 2 or j == low[1][1] - 1:
+                for ref, idx, val in pending:
+                    ref[idx] = val
+                pending = []
         return carry
 
-    lax.fori_loop(low[0][0], low[0][1], lower, 0)
-
-    def total(i, j):
-        e = e_at(i, j)
-        ezp = jnp.where(last, 0.0, up(e, s))
-        ezm = jnp.where(first, 0.0, down(e, s))
-        ex, ey = e_at(i - 1, j), e_at(i, j - 1)
-        d = half * (ex + e_at(i + 1, j) + ey + e_at(i, j + 1) + ezm + ezp + 6.0 * e)
-        return e, (ex, ey, ezm), d
-
-    def middle(i, carry):
-        for j in range(*mid[1]):
-            f = f_at(i, j)
-            _, _, d = total(i, j)
-            dm[i, j] = f * d + (1.0 - f)
+    loop(low[0][0], low[0][1], lower, unroll)
+
+    def smoother(i, carry):
+        pending = []
+        for j in range(*inv[1]):
+            e, f = e_at(i, j), f_at(i, j)
+            ezp = jnp.where(last, 0.0, up(e, s))
+            ezm = jnp.where(first, 0.0, down(e, s))
+            ex, ey = e_at(i - 1, j), e_at(i, j - 1)
+            d = half * (ex + e_at(i + 1, j) + ey + e_at(i, j + 1) + ezm + ezp + 6.0 * e)
+            pending.append((dm, (i, j), f * d + (1.0 - f)))
+            for c, below in enumerate((ex, ey, ezm)):
+                diag = jnp.where(e > 0.0, d + LAM * (e + below), 1.0)
+                dinv = jnp.where(e > 0.0, f / diag + (1.0 - f), 0.0)
+                pending.append((ad, (c, i, j), STEP_A * dinv))
+                pending.append((bd, (c, i, j), STEP_B * dinv))
+            if j % 3 == 2 or j == inv[1][1] - 1:
+                for ref, idx, val in pending:
+                    ref[idx] = val
+                pending = []
         return carry
 
-    lax.fori_loop(mid[0][0], mid[0][1], middle, 0)
-
-    def smoother(i, carry):
-        for j in range(*inv[1]):
-            f = f_at(i, j)
-            e, below, d = total(i, j)
+    loop(inv[0][0], inv[0][1], smoother, unroll)
+
+
+def sweep(v, s, xr, yr, co, w, emit, chunk, unroll):
+    kx, ky, kzp, kzm, dm, cw, cf, ff = co[:8]
+    wmask = lanes() < s
+
+    def spread(i, j, centre, ahead_x, ahead_y, ahead_z):
+        total = centre[0] + centre[1] + centre[2]
+        return cw[0, i, j] * ahead_x + cw[1, i, j] * ahead_y + cw[2, i, j] * ahead_z - cf[i, j] * total
+
+    def at(i, j):
+        return [v[c, i, j] for c in range(3)]
+
+    before = xr[0] - 1
+    stores = []
+    for j in range(*yr):
+        centre = at(before, j)
+        stores.append((j, spread(before, j, centre, v[0, before + 1, j], v[1, before, j + 1], up(centre[2], s))))
+    for j, val in stores:
+        w[before, j] = val
+
+    def body(i, carry):
+        j0 = yr[0] - 1
+        prev = at(i, j0)
+        here = at(i, yr[0])
+        wprev = spread(i, j0, prev, v[0, i + 1, j0], here[1], up(prev[2], s))
+        kyprev = ky[i, j0]
+        for ja in range(yr[0], yr[1], chunk):
+            rows, ws = {}, []
+            for j in range(ja, min(ja + chunk, yr[1])):
+                nxt = at(i, j + 1)
+                ahead = [v[c, i + 1, j] for c in range(3)]
+                zp = [up(here[c], s) for c in range(3)]
+                zm = [down(here[c], s) for c in range(3)]
+                wc = spread(i, j, here, ahead[0], nxt[1], zp[2])
+                below = (w[i - 1, j], wprev, jnp.where(wmask, 0.0, down(wc, s)))
+                k = (kx[i, j], kx[i - 1, j], ky[i, j], kyprev, kzp[i, j], kzm[i, j])
+                f, d = ff[i, j], dm[i, j]
+                out = []
+                for c in range(3):
+                    one = d * here[c] + f * (below[c] - wc)
+                    two = k[0] * ahead[c] + k[1] * v[c, i - 1, j]
+                    three = k[2] * nxt[c] + k[3] * prev[c]
+                    four = k[4] * zp[c] + k[5] * zm[c]
+                    out.append((here[c], (one - two) - (three + four)))
+                rows[j] = out
+                ws.append((j, wc))
+                prev, here, wprev, kyprev = here, nxt, wc, k[2]
+            pending = emit(i, rows)
+            for j, val in ws:
+                w[i, j] = val
+            for ref, idx, val in pending:
+                ref[idx] = val
+        return carry
+
+    loop(xr[0], xr[1], body, unroll)
+
+
+def loop(lo, hi, body, unroll):
+    if unroll:
+        for i in range(lo, hi):
+            body(i, 0)
+    else:
+        lax.fori_loop(lo, hi, body, 0)
+
+
+def smooth(v, s, xr, yr, co, w, rhs, step, out, chunk=4, unroll=False):
+    def emit(i, rows):
+        return [
+            (out, (c, i, j), vc + step[c, i, j] * (rhs[c, i, j] - av))
+            for j, vals in rows.items()
+            for c, (vc, av) in enumerate(vals)
+        ]
+
+    sweep(v, s, xr, yr, co, w, emit, chunk, unroll)
+
+
+def restrict(v, s, xr, yr, co, w, rhs, part, coarse, unroll=False):
+    def emit(i, rows):
+        pending = []
+        for j in list(rows)[::2]:
             for c in range(3):
-                diag = jnp.where(e > 0.0, d + LAM * (e + below[c]), 1.0)
-                dinv = jnp.where(e > 0.0, f / diag + (1.0 - f), 0.0)
-                ad[c, i, j] = STEP_A * dinv
-                bd[c, i, j] = STEP_B * dinv
-        return carry
-
-    lax.fori_loop(inv[0][0], inv[0][1], smoother, 0)
-
-
-def divergence(v, s, xr, yr, co, w):
-    cw, cf = co[5], co[6]
-
-    def body(i, carry):
-        for j in range(yr[0] - 1, yr[1]):
-            a, b, c = v[0, i, j], v[1, i, j], v[2, i, j]
-            w[i, j] = (
-                cw[0, i, j] * v[0, i + 1, j]
-                + cw[1, i, j] * v[1, i, j + 1]
-                + cw[2, i, j] * up(c, s)
-                - cf[i, j] * (a + b + c)
-            )
-        return carry
-
-    lax.fori_loop(xr[0] - 1, xr[1], body, 0)
-
-
-def plane(v, s, i, j, co, w, wmask):
-    kx, ky, kzp, kzm, dm, _, _, ff = co[:8]
-    wc = w[i, j]
-    wz = jnp.where(wmask, 0.0, down(wc, s))
-    below = (w[i - 1, j], w[i, j - 1], wz)
-    f = ff[i, j]
-    k = (kx[i, j], kx[i - 1, j], ky[i, j], ky[i, j - 1], kzp[i, j], kzm[i, j])
-    out = []
+                total = (rhs[c, i, j] - rows[j][c][1]) + (rhs[c, i, j + 1] - rows[j + 1][c][1])
+                pending.append((part, (c, i - xr[0], (j - yr[0]) // 2), total))
+        return pending
+
+    sweep(v, s, xr, yr, co, w, emit, 4, unroll)
+    pending = []
     for c in range(3):
-        vc = v[c, i, j]
-        lap = dm[i, j] * vc
-        lap -= k[0] * v[c, i + 1, j] + k[1] * v[c, i - 1, j]
-        lap -= k[2] * v[c, i, j + 1] + k[3] * v[c, i, j - 1]
-        lap -= k[4] * up(vc, s) + k[5] * down(vc, s)
-        out.append((vc, lap + f * (below[c] - wc)))
-    return out
-
-
-def apply(v, s, xr, yr, co, w, emit):
-    divergence(v, s, xr, yr, co, w)
-    wmask = lanes() < s
-
-    def body(i, carry):
-        for j in range(*yr):
-            for c, (vc, av) in enumerate(plane(v, s, i, j, co, w, wmask)):
-                emit(c, i, j, vc, av)
-        return carry
-
-    lax.fori_loop(xr[0], xr[1], body, 0)
-
-
-def smooth(v, s, xr, yr, co, w, rhs, step, out):
-    def emit(c, i, j, vc, av):
-        out[c, i, j] = vc + step[c, i, j] * (rhs[c, i, j] - av)
-
-    apply(v, s, xr, yr, co, w, emit)
-
-
-def restrict(v, s, xr, yr, co, w, rhs, coarse):
-    divergence(v, s, xr, yr, co, w)
-    wmask = lanes() < s
-
-    def body(q, carry):
-        for y2 in range((yr[1] - yr[0]) // 2):
-            acc = [None] * 3
-            for a in range(2):
-                for b in range(2):
-                    i, j = xr[0] + 2 * q + a, yr[0] + 2 * y2 + b
-                    for c, (_, av) in enumerate(plane(v, s, i, j, co, w, wmask)):
-                        rem = rhs[c, i, j] - av
-                        acc[c] = rem if acc[c] is None else acc[c] + rem
-            for c in range(3):
-                coarse[c, q, y2] = pair_sum(acc[c], s)
-        return carry
-
-    lax.fori_loop(0, (xr[1] - xr[0]) // 2, body, 0)
+        for q in range((xr[1] - xr[0]) // 2):
+            for y2 in range((yr[1] - yr[0]) // 2):
+                pending.append(((c, q, y2), pair_sum(part[c, 2 * q, y2] + part[c, 2 * q + 1, y2], s)))
+    for idx, val in pending:
+        coarse[idx] = val
 
 
 def column(m, i):
     picked = jnp.where(lanes() == subl(), row(m[i : i + 1, :]), 0.0)
     return row(jnp.sum(picked, axis=1, keepdims=True))
+
+
+def tree(terms):
+    while len(terms) > 1:
+        terms = [sum(terms[k : k + 2]) for k in range(0, len(terms), 2)]
+    return terms[0]
 
 
 def mm(a, b):
@@ -224,7 +249,7 @@
     kx3, ky3, kzp3, kzm3, dm3, cw3, cf3, ff3, ad3, bd3,
     t2, g2r, x2r, ecr, g2u, b1, b2, b3, b4, w2, e2u,
     t3, g3r, g3u, c1, c2, w3,
-    gram, ps1, ps2, mats, raw,
+    gram, ps1, ps2, mats, raw, part,
     send, recv, psend, precv,
 ):
     gx, gy = lax.axis_index("gx"), lax.axis_index("gy")
@@ -268,10 +293,16 @@
     def e2_refs(dx, dy):
         return e2b.at[2, 1], e2b.at[2 - dx, 1 - dy]
 
-    def halo(source, target, h):
+    def halo(source, target, h, skip=0):
+        def side(d, other, n):
+            if d == 0:
+                return 0, H, n
+            near, far = (skip, h) if other == 0 else (0, h - 1 if other == d else h)
+            return (n - far, H - far, far - near) if d > 0 else (near, H + n + near, far - near)
+
         def refs(dx, dy):
-            sx, tx, nx = span(dx, NX, h, H)
-            sy, ty, ny = span(dy, NY, h, H)
+            sx, tx, nx = side(dx, dy, NX)
+            sy, ty, ny = side(dy, dx, NY)
             a = source.at[:, pl.ds(H + sx, nx), pl.ds(H + sy, ny)]
             return a, target.at[:, pl.ds(tx, nx), pl.ds(ty, ny)]
         return refs
@@ -312,16 +343,10 @@
     corners = [(dx, dy) for dx in (1, -1, 2, -2) for dy in (1, -1)]
     peers = jnp.int32(size_x + size_y - 2)
 
-    def greet_x(d, carry):
+    for d in range(1, size_x):
         pl.semaphore_signal(bar, inc=1, device_id=(lax.rem(gx + d, size_x), gy), device_id_type=MESH)
-        return carry
-
-    def greet_y(d, carry):
+    for d in range(1, size_y):
         pl.semaphore_signal(bar, inc=1, device_id=(gx, lax.rem(gy + d, size_y)), device_id_type=MESH)
-        return carry
-
-    lax.fori_loop(1, size_x, greet_x, 0)
-    lax.fori_loop(1, size_y, greet_y, 0)
     for d in corners:
         peers = peers + jnp.where(valid(*d), 1, 0)
 
@@ -368,18 +393,20 @@
             fx[i, j] = row(fb[bx, by, xl, yl : yl + 1, :])
     coefficients(
         1, lambda i, j: ex[i, j], lambda i, j: fx[i, j],
-        ((0, 9), (0, 13)), ((1, 9), (1, 13)), ((1, 9), (1, 13)), co1,
+        ((0, 9), (0, 13)), ((1, 9), (1, 13)), co1,
     )
 
     arrive(K_G, N8, halo(raw, raw, 2))
 
     def first_rhs(i, carry):
         for c in range(3):
+            pending = []
             for j in range(1, 13):
                 k = ((c * 8 + i - 1) * 12 + j - 1) * NC
                 total = fx[i, j] * (raw[c, i, j] + loadbuf[pl.ds(pl.multiple_of(k, NC), NC), :])
-                total = jnp.where(ex[i, j] > 0.0, total, 0.0)
-                g[0, c, i, j] = total
+                pending.append((j, jnp.where(ex[i, j] > 0.0, total, 0.0)))
+            for j, val in pending:
+                g[0, c, i, j] = val
         return carry
 
     lax.fori_loop(1, 9, first_rhs, 0)
@@ -390,13 +417,16 @@
     def unpack_field(packed, out, add=None):
         for c in range(3):
             for bx in range(3):
+                pending = []
                 for j in range(8):
                     for a, val in enumerate(unpack(packed[c, bx, j])):
                         i = 2 * bx + a
                         val = jnp.where(ad2[0, i, j] > 0.0, val, 0.0)
                         if add is not None:
                             val = val + add[c, i // 2 + 1, j // 2 + 1]
-                        out[c, i, j] = val
+                        pending.append(((c, i, j), val))
+                for idx, val in pending:
+                    out[idx] = val
 
     def pack_field(field, base, packed):
         for c in range(3):
@@ -408,30 +438,31 @@
         own = ((H, H + NX), (H, H + NY))
         one_out = ((H - 1, H + NX + 1), (H - 1, H + NY + 1))
         two_out = ((H - 2, H + NX + 2), (H - 2, H + NY + 2))
-        x_refs = halo(a2, xb.at[it], 3)
+        x_refs = halo(a2, xb.at[it], 3, 1)
         g2, x2, ec, g3 = g2r.at[it], x2r.at[it], ecr.at[it], g3r.at[it]
 
         @pl.when(it == 1)
         def _():
             def clean(i, c2_):
                 for c in range(3):
-                    for j in range(1, 13):
-                        rhs[c, i, j] = jnp.where(ex[i, j] > 0.0, rhs[c, i, j], 0.0)
+                    pending = [(j, jnp.where(ex[i, j] > 0.0, rhs[c, i, j], 0.0)) for j in range(1, 13)]
+                    for j, val in pending:
+                        rhs[c, i, j] = val
                 return c2_
             lax.fori_loop(1, 9, clean, 0)
 
         def first(i, c2_):
             for c in range(3):
-                for j in range(1, 13):
-                    a1[c, i, j] = ad[c, i, j] * rhs[c, i, j]
+                pending = [(j, ad[c, i, j] * rhs[c, i, j]) for j in range(1, 13)]
+                for j, val in pending:
+                    a1[c, i, j] = val
             return c2_
 
         lax.fori_loop(1, 9, first, 0)
-        smooth(a1, 1, *one_out, co1, w, rhs, bd, a2)
-        restrict(a2, 1, *own, co1, w, rhs, t2)
+        smooth(a1, 1, *one_out, co1, w, rhs, bd, a2, 5)
+        restrict(a2, 1, *own, co1, w, rhs, part, t2)
         pack_field(t2, (0, 0), g2)
         start(K_G2 + it, N8, coarse_refs(g2))
-        start(K_X2 + it, N8, x_refs)
 
         @pl.when(it == 0)
         def _():
@@ -447,11 +478,11 @@
             one[...] = jnp.ones((NC, NZ), F32)
             coefficients(
                 2, lambda i, j: e2x[i + 2, j + 2], lambda i, j: one[...],
-                ((0, 5), (0, 7)), ((1, 5), (1, 7)), ((0, 6), (0, 8)), co2,
+                ((0, 5), (0, 7)), ((0, 6), (0, 8)), co2,
             )
             coefficients(
                 4, lambda i, j: e3x[i, j], lambda i, j: one[...],
-                ((0, 4), (0, 5)), ((1, 4), (1, 5)), ((1, 4), (1, 5)), co3,
+                ((0, 4), (0, 5)), ((1, 4), (1, 5)), co3,
             )
 
         arrive(K_G2 + it, N8, coarse_refs(g2))
@@ -461,15 +492,16 @@
                 for j in range(8):
                     b1[c, i, j] = ad2[c, i, j] * g2u[c, i, j]
         own2, out2 = ((2, 4), (2, 6)), ((1, 5), (1, 7))
-        smooth(b1, 2, *out2, co2, w2, g2u, bd2, b2)
+        smooth(b1, 2, *out2, co2, w2, g2u, bd2, b2, 3)
         pack_field(b2, (2, 2), x2)
         start(K_X2C + it, N8, coarse_refs(x2))
-        restrict(b2, 2, *own2, co2, w2, g2u, t3)
+        restrict(b2, 2, *own2, co2, w2, g2u, part, t3)
         for c in range(3):
             r0, r1 = t3[c, 0, 0], t3[c, 0, 1]
             s0, s1 = ad3[c, 2, 2] * r0, ad3[c, 2, 3] * r1
             g3[c, 2, 1] = jnp.where(low2, jnp.where(even, r0, r1), jnp.where(even, s0, s1))
         start(K_G3 + it, N14, g3_refs(g3))
+        start(K_X2 + it, N8, x_refs)
         arrive(K_G3 + it, N14, g3_refs(g3))
         for c in range(3):
             for bx in range(5):
@@ -478,35 +510,39 @@
                         keep = e3x[bx, 2 * by + a] > 0.0
                         g3u[c, bx, 2 * by + a] = jnp.where(keep, jnp.where(low2, q, down(q, 2)), 0.0)
                         c1[c, bx, 2 * by + a] = jnp.where(keep, jnp.where(low2, up(q, 2), q), 0.0)
-        smooth(c1, 4, (1, 4), (1, 5), co3, w3, g3u, bd3, c2)
+        smooth(c1, 4, (1, 4), (1, 5), co3, w3, g3u, bd3, c2, 4)
         arrive(K_X2C + it, N8, coarse_refs(x2))
         unpack_field(x2, b3, add=c2)
-        smooth(b3, 2, *out2, co2, w2, g2u, bd2, b4)
-        smooth(b4, 2, *own2, co2, w2, g2u, ad2, b1)
+        smooth(b3, 2, *out2, co2, w2, g2u, bd2, b4, 3)
+        smooth(b4, 2, *own2, co2, w2, g2u, ad2, b1, 4)
         pack_field(b1, (2, 2), ec)
         start(K_EC + it, N8, coarse_refs(ec))
         arrive(K_EC + it, N8, coarse_refs(ec))
         unpack_field(ec, e2u)
         arrive(K_X2 + it, N8, x_refs)
 
-        def correct(i, rows, from_own):
+        def correct(i, from_own):
             for c in range(3):
+                pending = []
                 for j in range(AY):
-                    inner = from_own and H <= j < H + NY
+                    inner = from_own(j)
                     old = a2[c, i, j] if inner else xb[it, c, i, j]
                     keep = ex[i, j] > 0.0
                     e = e2u[c, (i + 1) // 2, (j + 1) // 2]
-                    a3[c, i, j] = jnp.where(keep, old + fx[i, j] * e, 0.0)
+                    pending.append((j, jnp.where(keep, old + fx[i, j] * e, 0.0)))
+                for j, val in pending:
+                    a3[c, i, j] = val
 
         for i in range(AX):
-            correct(i, None, H <= i < H + NX)
+            out = 0 if H <= i < H + NX else 1 if H - 1 <= i <= H + NX else 9
+            correct(i, lambda j: out + (not H <= j < H + NY) + 9 * (not H - 1 <= j <= H + NY) < 2)
         smooth(a3, 1, *two_out, co1, w, rhs, bd, a4)
-        smooth(a4, 1, *one_out, co1, w, rhs, ad, pv.at[it])
-
-        def keep_image(c, i, j, vc, av):
-            g[it + 1, c, i, j] = av
-
-        apply(pv.at[it], 1, *own, co1, w, keep_image)
+        smooth(a4, 1, *one_out, co1, w, rhs, ad, pv.at[it], 5)
+
+        def keep_image(i, rows):
+            return [(g, (it + 1, c, i, j), av) for j, vals in rows.items() for c, (_, av) in enumerate(vals)]
+
+        sweep(pv.at[it], 1, *own, co1, w, keep_image, 4, False)
 
         q_refs = halo(g.at[1], g.at[1], 2)
 
@@ -567,21 +603,12 @@
                 device_id=place(other), device_id_type=MESH,
             )
 
-        def go(d, carry):
+        for d in range(1, count):
             copy(d).start()
-            return carry
-
-        def take(d, carry):
+        for d in range(1, count):
             landing(d).wait_recv()
-            return carry
-
-        def done(d, carry):
+        for d in range(1, count):
             copy(d).wait_send()
-            return carry
-
-        lax.fori_loop(1, count, go, 0)
-        lax.fori_loop(1, count, take, 0)
-        lax.fori_loop(1, count, done, 0)
         out = buffer[0]
         for k in range(1, count):
             out = out + buffer[k]
@@ -614,19 +641,20 @@
         m1 = [mats[0, k] for k in range(NC)]
         m2 = [mats[1, k] for k in range(NC)]
         i = H + x
+        def blend(one, two, c, j):
+            terms = [row(one[c, i, j, k : k + 1, :]) * m1[k] for k in range(NC)]
+            other = [row(two[c, i, j, k : k + 1, :]) * m2[k] for k in range(NC)]
+            return tree(terms) - tree(other)
+
         for c in range(3):
+            pending = []
             for y in range(NY):
                 j = H + y
-                sol = jnp.zeros((NC, NZ), F32)
-                res = g[0, c, i, j]
-                for k in range(NC):
-                    sol = sol + row(pv[0, c, i, j, k : k + 1, :]) * m1[k]
-                    sol = sol - row(pv[1, c, i, j, k : k + 1, :]) * m2[k]
-                    res = res - row(g[1, c, i, j, k : k + 1, :]) * m1[k]
-                    res = res + row(g[2, c, i, j, k : k + 1, :]) * m2[k]
                 at = pl.ds((c * NC * NX + x) * NY + y, NC, stride=NX * NY)
-                xo[at, :] = sol
-                ro[at, :] = res
+                pending.append((xo, at, blend(pv.at[0], pv.at[1], c, j)))
+                pending.append((ro, at, g[0, c, i, j] - blend(g.at[1], g.at[2], c, j)))
+            for ref, at, val in pending:
+                ref[at, :] = val
         return carry
 
     lax.fori_loop(0, NX, finish, 0)
@@ -652,7 +680,7 @@
     scratch += [vm(3, 2, 4), vm(2, 3, 3, 8), vm(2, 3, 3, 8), vm(2, 3, 3, 8)]
     scratch += [vm(3, 6, 8)] * 5 + [vm(6, 8), vm(3, 6, 8)]
     scratch += [vm(3, 1, 2), vm(2, 3, 5, 3), vm(3, 5, 6), vm(3, 5, 6), vm(3, 5, 6), vm(5, 6)]
-    scratch += [vm(2), vm(size_y), vm(size_x), vm(2, NC), vm(3, AX, AY)]
+    scratch += [vm(2), vm(size_y), vm(size_x), vm(2, NC), vm(3, AX, AY), vm(3, NX, 4)]
     sems = pltpu.SemaphoreType.DMA
     scratch += [sems((KINDS, len(N14))), sems((KINDS, len(N14))), sems((size_x + size_y,)), sems((size_x + size_y,))]
     spec = pl.BlockSpec(memory_space=pltpu.VMEM)

time: 137 us -> 116 us (0.85)
  Pallas kernels: 133 us -> 113 us
    pallas_call x1, Pallas kernels: 133 us -> 113 us  [on_device(): pl.pallas_call(functools.partial(kernel, size_x, size_y), out_shape=(shap...]
where the time goes in v2:
time: 116 us
  Pallas kernels  113 us (97%)
  local copies, waits for them, and re-layouts  2.57 us (2%)
    pallas_call x1, Pallas kernels, on_device(): pl.pallas_call(functools.partial(kernel, size_x, size_y), out_shape=(shap...  113 us
    unnamed x4, local copies, waits for them, and re-layouts  2.57 us

profile of v2, /device:TPU:1, one launch (start us, length us, event | category | flops | bytes accessed | tf_op | source)
XLA Modules:
  0.0 115.9 jit_solution(3346689806512325173)
XLA Ops:
  0.6 112.7 %block_pcg.1 = (f32[768,128]{1,0:T(8,128)}, f32[768,128]{1,0:T(8,128)}) custom-call(f32[768,128]{1,0:T(8,128)} %bitcast.3, s32[4,8,128]{2,1,0:T(8,128)} %dens.1, s32[4,8,128]{2,1,0:T(8,128)} %mask.1, s32[8,64]{1,0:T(8,128)} %nodes.1, f32[3,8,64]{2,1,0:T(8,128)} %forces.1), custom_call_target="tpu_custom_call" | custom-call | tf_op jit(solution)/shard_map/block_pcg/pallas_call | solution.py:688
  113.3 0.0 copy-start
  113.3 1.8 %copy.9 = f32[3,8,4,8,128]{4,3,2,1,0:T(8,128)} copy(f32[3,8,4,8,128]{4,3,2,1,0:T(8,128)} %bitcast.5) | data formatting | bytes 786432
  115.1 0.0 copy-done
  115.1 0.7 copy.10
Async XLA Ops:
  113.3 1.8 %copy-start = (f32[768,128]{1,0:T(8,128)S(1)}, f32[768,128]{1,0:T(8,128)}, u32[]{:S(2)}) copy-start(f32[768,128]{1,0:T(8,128)} %get-tuple-element.5) | copy-start | bytes 1179652

commit v3 on v2

--- a/solution.py
+++ b/solution.py
@@ -20,11 +20,16 @@
 NX, NY, NC, NZ, LOADS = 4, 8, 8, 128, 64
 H = 3
 AX, AY = NX + 2 * H, NY + 2 * H
-N8 = [(1, 0), (-1, 0), (0, 1), (0, -1), (1, 1), (1, -1), (-1, 1), (-1, -1)]
-N14 = [(dx, dy) for dx in (1, -1, 2, -2, 0) for dy in (0, 1, -1) if (dx, dy) != (0, 0)]
+N8 = [(1, -1), (-1, 1), (1, 1), (-1, -1), (1, 0), (-1, 0), (0, 1), (0, -1)]
+N14 = [(dx, dy) for dx in (2, -2, 1, -1, 0) for dy in (1, -1, 0) if (dx, dy) != (0, 0)]
 
 K_E, K_F, K_E2, K_G, K_X2, K_G2, K_X2C, K_G3, K_EC = 0, 1, 2, 3, 5, 7, 9, 11, 13
 KINDS = 15
+PIECES = 4
+
+
+def far_first(count):
+    return sorted(range(1, count), key=lambda d: abs(d - count / 2))
 
 
 def lanes():
@@ -61,7 +66,7 @@
 
 
 def coefficients(s, e_at, f_at, low, inv, co, unroll=False):
-    kx, ky, kzp, kzm, dm, cw, cf, ff, ad, bd = co
+    kx, ky, kzp, fup, dm, cw, cf, ff, ad, bd = co
     last = lanes() >= NZ - s
     first = lanes() < s
     half = 0.5 * MU
@@ -72,15 +77,14 @@
             e, f = e_at(i, j), f_at(i, j)
             fx, fy = f_at(i + 1, j), f_at(i, j + 1)
             fzp = jnp.where(last, 0.0, up(f, s))
-            fzm = jnp.where(first, 0.0, down(f, s))
-            ezp, ezm = up(e, s), down(e, s)
+            ezp = up(e, s)
             le = LAM * e
             hf = half * f
             pending += [
                 (kx, (i, j), (e + e_at(i + 1, j)) * (hf * fx)),
                 (ky, (i, j), (e + e_at(i, j + 1)) * (hf * fy)),
                 (kzp, (i, j), (e + ezp) * (hf * fzp)),
-                (kzm, (i, j), (ezm + e) * (hf * fzm)),
+                (fup, (i, j), fzp),
                 (cw, (0, i, j), le * fx),
                 (cw, (1, i, j), le * fy),
                 (cw, (2, i, j), le * fzp),
@@ -118,9 +122,62 @@
     loop(inv[0][0], inv[0][1], smoother, unroll)
 
 
+def compact_coefficients(e_ref, f_ref, co, ex, fx):
+    kx, ky, kzp, fup, dm, cw, cf, ff, ad, bd = co
+    half = 0.5 * MU
+    wide = (16, NZ)
+    lane = lax.broadcasted_iota(jnp.int32, wide, 1)
+
+    def zup(v):
+        return jnp.where(lane == NZ - 1, 0.0, pltpu.roll(v, NZ - 1, 1))
+
+    def ynext(v):
+        return pltpu.roll(v, 15, 0)
+
+    def plane(i, carry):
+        e, f, e1, f1 = e_ref[i], f_ref[i], e_ref[i + 1], f_ref[i + 1]
+        fy, fz = ynext(f), zup(f)
+        le, hf = LAM * e, half * f
+        ahead = (
+            (ex, (i,), e), (fx, (i,), f),
+            (kx, (i,), (e + e1) * (hf * f1)),
+            (ky, (i,), (e + ynext(e)) * (hf * fy)),
+            (kzp, (i,), (e + zup(e)) * (hf * fz)),
+            (fup, (i,), fz), (cw, (0, i), le * f1), (cw, (1, i), le * fy),
+            (cw, (2, i), le * fz), (cf, (i,), le * f), (ff, (i,), f),
+        )
+        for ref, at, val in ahead:
+            for j in range(AY):
+                ref[at + (j,)] = row(val[j : j + 1, :])
+        return carry
+
+    lax.fori_loop(0, AX - 1, plane, 0)
+    for ref, source in ((ex, e_ref), (fx, f_ref)):
+        last = source[AX - 1]
+        for j in range(AY):
+            ref[AX - 1, j] = row(last[j : j + 1, :])
+
+    def smoother(i, carry):
+        e, f = e_ref[i], f_ref[i]
+        ey = pltpu.roll(e, 1, 0)
+        ez = jnp.where(lane == 0, 0.0, pltpu.roll(e, 1, 1))
+        eb = e_ref[i - 1]
+        d = half * (eb + e_ref[i + 1] + ey + ynext(e) + ez + zup(e) + 6.0 * e)
+        out = [(dm, (i,), f * d + (1.0 - f))]
+        for c, below in enumerate((eb, ey, ez)):
+            diag = jnp.where(e > 0.0, d + LAM * (e + below), 1.0)
+            dinv = jnp.where(e > 0.0, f / diag + (1.0 - f), 0.0)
+            out += [(ad, (c, i), STEP_A * dinv), (bd, (c, i), STEP_B * dinv)]
+        for ref, at, val in out:
+            for j in range(1, AY - 1):
+                ref[at + (j,)] = row(val[j : j + 1, :])
+        return carry
+
+    lax.fori_loop(1, AX - 1, smoother, 0)
+
+
 def sweep(v, s, xr, yr, co, w, emit, chunk, unroll):
-    kx, ky, kzp, kzm, dm, cw, cf, ff = co[:8]
-    wmask = lanes() < s
+    kx, ky, kzp, fup, dm, cw, cf, ff = co[:8]
 
     def spread(i, j, centre, ahead_x, ahead_y, ahead_z):
         total = centre[0] + centre[1] + centre[2]
@@ -149,18 +206,20 @@
                 nxt = at(i, j + 1)
                 ahead = [v[c, i + 1, j] for c in range(3)]
                 zp = [up(here[c], s) for c in range(3)]
-                zm = [down(here[c], s) for c in range(3)]
                 wc = spread(i, j, here, ahead[0], nxt[1], zp[2])
-                below = (w[i - 1, j], wprev, jnp.where(wmask, 0.0, down(wc, s)))
-                k = (kx[i, j], kx[i - 1, j], ky[i, j], kyprev, kzp[i, j], kzm[i, j])
+                k = (kx[i, j], kx[i - 1, j], ky[i, j], kyprev, kzp[i, j])
                 f, d = ff[i, j], dm[i, j]
+                fwc = f * wc
+                gain = (f * w[i - 1, j] - fwc, f * wprev - fwc, -fwc)
                 out = []
                 for c in range(3):
-                    one = d * here[c] + f * (below[c] - wc)
+                    one = d * here[c] + gain[c]
                     two = k[0] * ahead[c] + k[1] * v[c, i - 1, j]
                     three = k[2] * nxt[c] + k[3] * prev[c]
-                    four = k[4] * zp[c] + k[5] * zm[c]
-                    out.append((here[c], (one - two) - (three + four)))
+                    back = k[4] * here[c]
+                    if c == 2:
+                        back = back - fup[i, j] * wc
+                    out.append((here[c], (one - two) - (three + k[4] * zp[c]) - down(back, s)))
                 rows[j] = out
                 ws.append((j, wc))
                 prev, here, wprev, kyprev = here, nxt, wc, k[2]
@@ -212,9 +271,22 @@
         coarse[idx] = val
 
 
-def column(m, i):
-    picked = jnp.where(lanes() == subl(), row(m[i : i + 1, :]), 0.0)
-    return row(jnp.sum(picked, axis=1, keepdims=True))
+def pick(col, k):
+    return row(col[k : k + 1, :])
+
+
+def columns(m, base):
+    return [row(m[:, base + k : base + k + 1]) for k in range(NC)]
+
+
+def flip(a):
+    out = []
+    for k in range(NC):
+        col = pick(a[0], k)
+        for i in range(1, NC):
+            col = jnp.where(subl() == i, pick(a[i], k), col)
+        out.append(col)
+    return out
 
 
 def tree(terms):
@@ -224,19 +296,26 @@
 
 
 def mm(a, b):
-    return sum(row(a[:, k : k + 1]) * row(b[k : k + 1, :]) for k in range(NC))
-
-
-def mtm(a, b):
-    return sum(column(a, k) * row(b[k : k + 1, :]) for k in range(NC))
+    return [tree([a[k] * pick(col, k) for k in range(NC)]) for col in b]
+
+
+def plus(a, b):
+    return [x + y for x, y in zip(a, b)]
+
+
+def minus(a, b):
+    return [x - y for x, y in zip(a, b)]
 
 
 def solve(matrix, rhs):
-    aug = jnp.where(lanes() < NC, matrix, pltpu.roll(rhs, NC, 1))
+    left, right = list(matrix), list(rhs)
     for k in range(NC):
-        scaled = row(aug[k : k + 1, :]) / row(aug[k : k + 1, k : k + 1])
-        aug = jnp.where(subl() == k, scaled, aug - row(aug[:, k : k + 1]) * scaled)
-    return up(aug, NC)
+        inverse = 1.0 / pick(left[k], k)
+        for cols, first in ((left, k + 1), (right, 0)):
+            for j in range(first, NC):
+                scaled = pick(cols[j], k) * inverse
+                cols[j] = jnp.where(subl() == k, scaled, cols[j] - left[k] * scaled)
+    return right
 
 
 def kernel(
@@ -244,18 +323,18 @@
     src, dens, mask, nodes, forces, xo, ro,
     eb, fb, e2b, ex, fx, e2x, e3x, one,
     g, pv, a1, a2, a3, a4, xb, w, loadbuf,
-    kx, ky, kzp, kzm, dm, cw, cf, ff, ad, bd,
-    kx2, ky2, kzp2, kzm2, dm2, cw2, cf2, ff2, ad2, bd2,
-    kx3, ky3, kzp3, kzm3, dm3, cw3, cf3, ff3, ad3, bd3,
+    kx, ky, kzp, fup, dm, cw, cf, ff, ad, bd,
+    kx2, ky2, kzp2, fup2, dm2, cw2, cf2, ff2, ad2, bd2,
+    kx3, ky3, kzp3, fup3, dm3, cw3, cf3, ff3, ad3, bd3,
     t2, g2r, x2r, ecr, g2u, b1, b2, b3, b4, w2, e2u,
     t3, g3r, g3u, c1, c2, w3,
-    gram, ps1, ps2, mats, raw, part,
-    send, recv, psend, precv,
+    gram, ps1, ps2, mats, raw, part, ec0, fc0,
+    send, recv, psend, precv, flat_src, fetched,
 ):
     gx, gy = lax.axis_index("gx"), lax.axis_index("gy")
-    co1 = (kx, ky, kzp, kzm, dm, cw, cf, ff, ad, bd)
-    co2 = (kx2, ky2, kzp2, kzm2, dm2, cw2, cf2, ff2, ad2, bd2)
-    co3 = (kx3, ky3, kzp3, kzm3, dm3, cw3, cf3, ff3, ad3, bd3)
+    co1 = (kx, ky, kzp, fup, dm, cw, cf, ff, ad, bd)
+    co2 = (kx2, ky2, kzp2, fup2, dm2, cw2, cf2, ff2, ad2, bd2)
+    co3 = (kx3, ky3, kzp3, fup3, dm3, cw3, cf3, ff3, ad3, bd3)
     even = (lanes() & 1) == 0
     low2 = (lanes() & 2) == 0
 
@@ -288,7 +367,11 @@
                 message(kind, k, d, refs).wait_send()
 
     def boxes(ref):
-        return lambda dx, dy: (ref.at[1, 1], ref.at[1 - dx, 1 - dy])
+        def refs(dx, dy):
+            n = NX if dx == 0 else 2 if dx == dy else 3
+            at = pl.ds(NX - n if dx > 0 else 0, n)
+            return ref.at[1, 1, at], ref.at[1 - dx, 1 - dy, at]
+        return refs
 
     def e2_refs(dx, dy):
         return e2b.at[2, 1], e2b.at[2 - dx, 1 - dy]
@@ -309,13 +392,15 @@
 
     def coarse_refs(ref):
         def refs(dx, dy):
-            sy, ty, ny = span(dy, 4, 2, 2)
+            sy, ty, ny = span(dy, 4, 1 if dx == dy else 2, 2)
             return ref.at[:, 1, pl.ds(2 + sy, ny)], ref.at[:, 1 - dx, pl.ds(ty, ny)]
         return refs
 
     def g3_refs(ref):
         return lambda dx, dy: (ref.at[:, 2, 1], ref.at[:, 2 - dx, 1 - dy])
 
+    fetch = pltpu.make_async_copy(src, flat_src, fetched)
+    fetch.start()
     zero3 = jnp.zeros((NX, NY, NZ), F32)
     for bx in range(3):
         for by in range(3):
@@ -324,6 +409,20 @@
     for bx in range(5):
         for by in range(3):
             e2b[bx, by] = jnp.zeros((NC, NZ), F32)
+    bar = pltpu.get_barrier_semaphore()
+    corners = [(dx, dy) for dx in (1, -1, 2, -2) for dy in (1, -1)]
+    peers = jnp.int32(size_x + size_y - 2)
+
+    for d in far_first(size_x):
+        pl.semaphore_signal(bar, inc=1, device_id=(lax.rem(gx + d, size_x), gy), device_id_type=MESH)
+    for d in far_first(size_y):
+        pl.semaphore_signal(bar, inc=1, device_id=(gx, lax.rem(gy + d, size_y)), device_id_type=MESH)
+    for d in corners:
+        peers = peers + jnp.where(valid(*d), 1, 0)
+
+        @pl.when(valid(*d))
+        def _():
+            pl.semaphore_signal(bar, inc=1, device_id=(gx + d[0], gy + d[1]), device_id_type=MESH)
     for x in range(NX):
         rel = (dens[x].astype(F32) + 1.0) / CLASSES
         eb[1, 1, x] = MIN_MODULUS + (1.0 - MIN_MODULUS) * rel * rel * rel
@@ -334,25 +433,12 @@
         halves.append(0.25 * pair_sum(t + pltpu.roll(t, NY - 1, 0), 1))
     e2b[2, 1] = jnp.where((subl() & 1) == 0, halves[0], pltpu.roll(halves[1], 1, 0))
 
+    fetch.wait()
     for c in range(3):
         for x in range(NX):
             for y in range(NY):
-                raw[c, H + x, H + y] = src[pl.ds((c * NC * NX + x) * NY + y, NC, stride=NX * NY), :]
-
-    bar = pltpu.get_barrier_semaphore()
-    corners = [(dx, dy) for dx in (1, -1, 2, -2) for dy in (1, -1)]
-    peers = jnp.int32(size_x + size_y - 2)
-
-    for d in range(1, size_x):
-        pl.semaphore_signal(bar, inc=1, device_id=(lax.rem(gx + d, size_x), gy), device_id_type=MESH)
-    for d in range(1, size_y):
-        pl.semaphore_signal(bar, inc=1, device_id=(gx, lax.rem(gy + d, size_y)), device_id_type=MESH)
-    for d in corners:
-        peers = peers + jnp.where(valid(*d), 1, 0)
-
-        @pl.when(valid(*d))
-        def _():
-            pl.semaphore_signal(bar, inc=1, device_id=(gx + d[0], gy + d[1]), device_id_type=MESH)
+                raw[c, H + x, H + y] = flat_src[pl.ds((c * NC * NX + x) * NY + y, NC, stride=NX * NY), :]
+
     pl.semaphore_wait(bar, peers)
 
     start(K_E, N8, boxes(eb))
@@ -387,14 +473,12 @@
     arrive(K_E, N8, boxes(eb))
     arrive(K_F, N8, boxes(fb))
     for i in range(AX):
-        for j in range(AY):
-            bx, xl, by, yl = (i + 1) // 4, (i + 1) % 4, (j + 5) // 8, (j + 5) % 8
-            ex[i, j] = row(eb[bx, by, xl, yl : yl + 1, :])
-            fx[i, j] = row(fb[bx, by, xl, yl : yl + 1, :])
-    coefficients(
-        1, lambda i, j: ex[i, j], lambda i, j: fx[i, j],
-        ((0, 9), (0, 13)), ((1, 9), (1, 13)), co1,
-    )
+        bx, xl = (i + 1) // 4, (i + 1) % 4
+        for source, flat in ((eb, ec0), (fb, fc0)):
+            flat[i, 0:3] = source[bx, 0, xl, 5:8]
+            flat[i, 3:11] = source[bx, 1, xl]
+            flat[i, 11:14] = source[bx, 2, xl, 0:3]
+    compact_coefficients(ec0, fc0, co1, ex, fx)
 
     arrive(K_G, N8, halo(raw, raw, 2))
 
@@ -432,6 +516,13 @@
         for c in range(3):
             for j in range(4):
                 packed[c, 1, 2 + j] = jnp.where(even, field[c, base[0], base[1] + j], field[c, base[0] + 1, base[1] + j])
+
+    def drain(it):
+        sent(K_X2 + it, N8, halo(a2, xb.at[it], 3, 1))
+        sent(K_G2 + it, N8, coarse_refs(g2r.at[it]))
+        sent(K_X2C + it, N8, coarse_refs(x2r.at[it]))
+        sent(K_G3 + it, N14, g3_refs(g3r.at[it]))
+        sent(K_EC + it, N8, coarse_refs(ecr.at[it]))
 
     def cycle(it, carry):
         rhs = g.at[it]
@@ -489,8 +580,9 @@
         unpack_field(g2, g2u)
         for c in range(3):
             for i in range(6):
-                for j in range(8):
-                    b1[c, i, j] = ad2[c, i, j] * g2u[c, i, j]
+                pending = [(j, ad2[c, i, j] * g2u[c, i, j]) for j in range(8)]
+                for j, val in pending:
+                    b1[c, i, j] = val
         own2, out2 = ((2, 4), (2, 6)), ((1, 5), (1, 7))
         smooth(b1, 2, *out2, co2, w2, g2u, bd2, b2, 3)
         pack_field(b2, (2, 2), x2)
@@ -504,12 +596,17 @@
         start(K_X2 + it, N8, x_refs)
         arrive(K_G3 + it, N14, g3_refs(g3))
         for c in range(3):
+            pending = []
             for bx in range(5):
                 for by in range(3):
                     for a, q in enumerate(unpack(g3[c, bx, by])):
-                        keep = e3x[bx, 2 * by + a] > 0.0
-                        g3u[c, bx, 2 * by + a] = jnp.where(keep, jnp.where(low2, q, down(q, 2)), 0.0)
-                        c1[c, bx, 2 * by + a] = jnp.where(keep, jnp.where(low2, up(q, 2), q), 0.0)
+                        j = 2 * by + a
+                        keep = e3x[bx, j] > 0.0
+                        if 1 <= bx <= 3 and 1 <= j <= 4:
+                            pending.append((g3u, (c, bx, j), jnp.where(keep, jnp.where(low2, q, down(q, 2)), 0.0)))
+                        pending.append((c1, (c, bx, j), jnp.where(keep, jnp.where(low2, up(q, 2), q), 0.0)))
+            for ref, idx, val in pending:
+                ref[idx] = val
         smooth(c1, 4, (1, 4), (1, 5), co3, w3, g3u, bd3, c2, 4)
         arrive(K_X2C + it, N8, coarse_refs(x2))
         unpack_field(x2, b3, add=c2)
@@ -571,23 +668,22 @@
 
         @pl.when(it == 0)
         def _():
+            drain(0)
             arrive(K_G + 1, N8, q_refs)
             sent(K_G + 1, N8, q_refs)
 
-        sent(K_X2 + it, N8, x_refs)
-        sent(K_G2 + it, N8, coarse_refs(g2))
-        sent(K_X2C + it, N8, coarse_refs(x2))
-        sent(K_G3 + it, N14, g3_refs(g3))
-        sent(K_EC + it, N8, coarse_refs(ec))
         return carry
 
     lax.fori_loop(0, 2, cycle, 0)
-    sent(K_E, N8, boxes(eb))
-    sent(K_F, N8, boxes(fb))
-    sent(K_G, N8, halo(raw, raw, 2))
-    sent(K_E2, N14, e2_refs)
-
-    def total(buffer, me, count, place, base):
+
+    def settle():
+        drain(1)
+        sent(K_E, N8, boxes(eb))
+        sent(K_F, N8, boxes(fb))
+        sent(K_G, N8, halo(raw, raw, 2))
+        sent(K_E2, N14, e2_refs)
+
+    def total(buffer, me, count, place, base, meanwhile=None):
         def copy(d):
             return pltpu.make_async_remote_copy(
                 src_ref=buffer.at[me], dst_ref=buffer.at[me],
@@ -603,9 +699,11 @@
                 device_id=place(other), device_id_type=MESH,
             )
 
-        for d in range(1, count):
+        for d in far_first(count):
             copy(d).start()
-        for d in range(1, count):
+        if meanwhile is not None:
+            meanwhile()
+        for d in far_first(count)[::-1]:
             landing(d).wait_recv()
         for d in range(1, count):
             copy(d).wait_send()
@@ -615,49 +713,60 @@
         return out
 
     ps1[gy] = jnp.where(lanes() < 2 * NC, gram[0], pltpu.roll(gram[1], 2 * NC, 1))
-    ps2[gx] = total(ps1, gy, size_y, lambda k: (gx, k), 0)
+    ps2[gx] = total(ps1, gy, size_y, lambda k: (gx, k), 0, settle)
     sums = total(ps2, gx, size_x, lambda k: (k, gy), size_y)
 
-    rz = sums
-    qp = up(sums, NC)
-    ru = up(sums, 2 * NC)
-    qu = up(sums, 3 * NC)
-    wu = up(sums, 4 * NC)
-    eye = jnp.where(lanes() == subl(), 1.0, 0.0)
+    rz = columns(sums, 0)
+    qp = columns(sums, NC)
+    ru = columns(sums, 2 * NC)
+    qu = columns(sums, 3 * NC)
+    wu = columns(sums, 4 * NC)
     alpha = solve(qp, rz)
-    inverse = solve(rz, eye)
-    rz2 = rz - mm(ru, alpha) + mtm(alpha, mm(qu, alpha) - qp)
-    mix = eye + mm(inverse, rz2)
-    quw = mm(qu, alpha)
-    pq2 = mtm(mix, mtm(qp, mix) - quw) + mtm(alpha, mtm(wu, alpha) - mtm(qu, mix))
-    alpha2 = solve(pq2, rz2)
-    one_m = alpha + mm(mix, alpha2)
-    two_m = mm(alpha, alpha2)
-    for k in range(NC):
-        mats[0, k] = column(one_m, k)
-        mats[1, k] = column(two_m, k)
-
-    def finish(x, carry):
-        m1 = [mats[0, k] for k in range(NC)]
-        m2 = [mats[1, k] for k in range(NC)]
+    alpha_t = flip(alpha)
+    qua = mm(qu, alpha)
+    rz2 = plus(minus(rz, mm(ru, alpha)), mm(alpha_t, minus(qua, qp)))
+    mix = [jnp.where(subl() == k, col + 1.0, col) for k, col in enumerate(solve(rz, rz2))]
+    ahead = minus(mm(flip(qp), mix), qua)
+    behind = minus(mm(flip(wu), alpha), mm(flip(qu), mix))
+    alpha2 = solve(plus(mm(flip(mix), ahead), mm(alpha_t, behind)), rz2)
+    for q, m in enumerate((plus(alpha, mm(mix, alpha2)), mm(alpha, alpha2))):
+        for k, col in enumerate(flip(m)):
+            mats[q, k] = col
+
+    def finish(n, carry):
+        c, x = lax.div(n, NX), lax.rem(n, NX)
         i = H + x
-        def blend(one, two, c, j):
-            terms = [row(one[c, i, j, k : k + 1, :]) * m1[k] for k in range(NC)]
-            other = [row(two[c, i, j, k : k + 1, :]) * m2[k] for k in range(NC)]
-            return tree(terms) - tree(other)
-
-        for c in range(3):
-            pending = []
-            for y in range(NY):
-                j = H + y
-                at = pl.ds((c * NC * NX + x) * NY + y, NC, stride=NX * NY)
-                pending.append((xo, at, blend(pv.at[0], pv.at[1], c, j)))
-                pending.append((ro, at, g[0, c, i, j] - blend(g.at[1], g.at[2], c, j)))
-            for ref, at, val in pending:
-                ref[at, :] = val
+        for one, two, ref, base in ((pv.at[0], pv.at[1], xo, None), (g.at[1], g.at[2], ro, g.at[0])):
+            accs = [None] * NY
+            for k in range(NC):
+                m1, m2 = mats[0, k], mats[1, k]
+                for y in range(NY):
+                    j = H + y
+                    term = row(one[c, i, j, k : k + 1, :]) * m1 - row(two[c, i, j, k : k + 1, :]) * m2
+                    accs[y] = term if k == 0 else accs[y] + term
+            pending = [(y, acc if base is None else base[c, i, H + y] - acc) for y, acc in enumerate(accs)]
+            for y, val in pending:
+                ref[pl.ds((c * NC * NX + x) * NY + y, NC, stride=NX * NY), :] = val
         return carry
 
-    lax.fori_loop(0, NX, finish, 0)
+    lax.fori_loop(0, 3 * NX, finish, 0)
+
+
+def publish(a, b, out_a, out_b, stage, sem):
+    loads, stores = [], []
+    n = a.shape[0] // PIECES
+    for k in range(PIECES):
+        for q, (one, two) in enumerate(((a, out_a), (b, out_b))):
+            at = pl.ds(k * n, n)
+            loads.append(pltpu.make_async_copy(one.at[at], stage.at[q, at], sem.at[0, q, k]))
+            stores.append(pltpu.make_async_copy(stage.at[q, at], two.at[at], sem.at[1, q, k]))
+    for copy in loads:
+        copy.start()
+    for load, store in zip(loads, stores):
+        load.wait()
+        store.start()
+    for copy in stores:
+        copy.wait()
 
 
 def on_device(size_x, size_y, source_field, density_class, fixed_mask, load_nodes, load_forces):
@@ -681,14 +790,16 @@
     scratch += [vm(3, 6, 8)] * 5 + [vm(6, 8), vm(3, 6, 8)]
     scratch += [vm(3, 1, 2), vm(2, 3, 5, 3), vm(3, 5, 6), vm(3, 5, 6), vm(3, 5, 6), vm(5, 6)]
     scratch += [vm(2), vm(size_y), vm(size_x), vm(2, NC), vm(3, AX, AY), vm(3, NX, 4)]
+    scratch += [pltpu.VMEM((AX, 16, NZ), F32)] * 2
     sems = pltpu.SemaphoreType.DMA
     scratch += [sems((KINDS, len(N14))), sems((KINDS, len(N14))), sems((size_x + size_y,)), sems((size_x + size_y,))]
+    scratch += [pltpu.VMEM((rows, NZ), F32), sems(())]
     spec = pl.BlockSpec(memory_space=pltpu.VMEM)
     shape = jax.ShapeDtypeStruct((rows, NZ), F32)
     sol, res = pl.pallas_call(
         functools.partial(kernel, size_x, size_y),
         out_shape=(shape, shape),
-        in_specs=[spec] * 5,
+        in_specs=[pl.BlockSpec(memory_space=pl.ANY)] + [spec] * 4,
         out_specs=(spec, spec),
         scratch_shapes=scratch,
         compiler_params=pltpu.CompilerParams(
@@ -696,6 +807,15 @@
         ),
         name="block_pcg",
     )(source_field.reshape(rows, NZ), density_class, fixed_mask, load_nodes, load_forces)
+    whole = pl.BlockSpec(memory_space=pl.ANY)
+    sol, res = pl.pallas_call(
+        publish,
+        out_shape=(shape, shape),
+        in_specs=[whole] * 2,
+        out_specs=(whole, whole),
+        scratch_shapes=[pltpu.VMEM((2, rows, NZ), F32), sems((2, 2, PIECES))],
+        name="publish",
+    )(sol, res)
     return sol.reshape(source_field.shape), res.reshape(source_field.shape)
 
 

time: 116 us -> 107 us (0.922)
  Pallas kernels: 113 us -> 106 us
  local copies, waits for them, and re-layouts: 2.57 us -> 0 us
    pallas_call x1, Pallas kernels: 113 us -> 104 us  [on_device(): pl.pallas_call(functools.partial(kernel, size_x, size_y), out_shape=(shap...]
    unnamed x4 -> x0, local copies, waits for them, and re-layouts: 2.57 us -> none
    pallas_call x0 -> x1, Pallas kernels: none -> 1.99 us  [on_device(): pl.pallas_call(publish, out_shape=(shape, shape), in_specs=[whole] * 2, o...]
where the time goes in v3:
time: 107 us
  Pallas kernels  106 us (99%)
    pallas_call x1, Pallas kernels, on_device(): pl.pallas_call(functools.partial(kernel, size_x, size_y), out_shape=(shap...  104 us

profile of v3, /device:TPU:1, one launch (start us, length us, event | category | flops | bytes accessed | tf_op | source)
XLA Modules:
  0.0 107.0 jit_solution(18265933454591678908)
XLA Ops:
  0.6 104.4 %block_pcg.1 = (f32[768,128]{1,0:T(8,128)}, f32[768,128]{1,0:T(8,128)}) custom-call(f32[768,128]{1,0:T(8,128)} %bitcast.3, s32[4,8,128]{2,1,0:T(8,128)} %dens.1, s32[4,8,128]{2,1,0:T(8,128)} %mask.1, s32[8,64]{1,0:T(8,128)} %nodes.1, f32[3,8,64]{2,1,0:T(8,128)} %forces.1), custom_call_target="tpu_custom_call" | custom-call | tf_op jit(solution)/shard_map/block_pcg/pallas_call | solution.py:799
  105.0 2.0 %publish.1 = (f32[768,128]{1,0:T(8,128)}, f32[768,128]{1,0:T(8,128)}) custom-call(f32[768,128]{1,0:T(8,128)} %get-tuple-element.6.a, f32[768,128]{1,0:T(8,128)} %get-tuple-element.7.b), custom_call_target="tpu_custom_call" | custom-call | tf_op jit(solution)/shard_map/publish/pallas_call | solution.py:811

commit v4 on v3

--- a/solution.py
+++ b/solution.py
@@ -18,6 +18,7 @@
 F32 = jnp.float32
 
 NX, NY, NC, NZ, LOADS = 4, 8, 8, 128, 64
+NROWS = 3 * NC * NX * NY
 H = 3
 AX, AY = NX + 2 * H, NY + 2 * H
 N8 = [(1, -1), (-1, 1), (1, 1), (-1, -1), (1, 0), (-1, 0), (0, 1), (0, -1)]
@@ -271,22 +272,17 @@
         coarse[idx] = val
 
 
-def pick(col, k):
-    return row(col[k : k + 1, :])
-
-
-def columns(m, base):
-    return [row(m[:, base + k : base + k + 1]) for k in range(NC)]
-
-
-def flip(a):
-    out = []
-    for k in range(NC):
-        col = pick(a[0], k)
-        for i in range(1, NC):
-            col = jnp.where(subl() == i, pick(a[i], k), col)
-        out.append(col)
-    return out
+def pick(m, k):
+    return row(m[k : k + 1, :])
+
+
+def columns(m):
+    return [row(m[:, k : k + 1]) for k in range(NC)]
+
+
+def flipped(m):
+    diagonal = lanes() == subl()
+    return [row(jnp.sum(jnp.where(diagonal, pick(m, k), 0.0), axis=1, keepdims=True)) for k in range(NC)]
 
 
 def tree(terms):
@@ -295,32 +291,26 @@
     return terms[0]
 
 
-def mm(a, b):
-    return [tree([a[k] * pick(col, k) for k in range(NC)]) for col in b]
-
-
-def plus(a, b):
-    return [x + y for x, y in zip(a, b)]
-
-
-def minus(a, b):
-    return [x - y for x, y in zip(a, b)]
-
-
-def solve(matrix, rhs):
-    left, right = list(matrix), list(rhs)
+def mm(cols, m):
+    return tree([cols[k] * pick(m, k) for k in range(NC)])
+
+
+def solve(cols, rhs):
+    left = list(cols)
     for k in range(NC):
+        pivot_row = subl() == k
         inverse = 1.0 / pick(left[k], k)
-        for cols, first in ((left, k + 1), (right, 0)):
-            for j in range(first, NC):
-                scaled = pick(cols[j], k) * inverse
-                cols[j] = jnp.where(subl() == k, scaled, cols[j] - left[k] * scaled)
-    return right
+        for j in range(k + 1, NC):
+            scaled = pick(left[j], k) * inverse
+            left[j] = jnp.where(pivot_row, scaled, left[j] - left[k] * scaled)
+        scaled = pick(rhs, k) * inverse
+        rhs = jnp.where(pivot_row, scaled, rhs - left[k] * scaled)
+    return rhs
 
 
 def kernel(
     size_x, size_y,
-    src, dens, mask, nodes, forces, xo, ro,
+    src, dens_in, mask_in, nodes_in, forces_in, xo, ro,
     eb, fb, e2b, ex, fx, e2x, e3x, one,
     g, pv, a1, a2, a3, a4, xb, w, loadbuf,
     kx, ky, kzp, fup, dm, cw, cf, ff, ad, bd,
@@ -328,8 +318,8 @@
     kx3, ky3, kzp3, fup3, dm3, cw3, cf3, ff3, ad3, bd3,
     t2, g2r, x2r, ecr, g2u, b1, b2, b3, b4, w2, e2u,
     t3, g3r, g3u, c1, c2, w3,
-    gram, ps1, ps2, mats, raw, part, ec0, fc0,
-    send, recv, psend, precv, flat_src, fetched,
+    gram, ps1, ps2, mats, raw, pairs, ec0, fc0,
+    send, recv, psend, precv, flat_src, stage, stored, dens, mask, nodes, forces, fetched,
 ):
     gx, gy = lax.axis_index("gx"), lax.axis_index("gy")
     co1 = (kx, ky, kzp, fup, dm, cw, cf, ff, ad, bd)
@@ -399,8 +389,10 @@
     def g3_refs(ref):
         return lambda dx, dy: (ref.at[:, 2, 1], ref.at[:, 2 - dx, 1 - dy])
 
-    fetch = pltpu.make_async_copy(src, flat_src, fetched)
-    fetch.start()
+    inputs = ((dens_in, dens), (mask_in, mask), (src, flat_src.at[pl.ds(0, NROWS)]), (nodes_in, nodes), (forces_in, forces))
+    fetch = [pltpu.make_async_copy(a, b, fetched.at[k]) for k, (a, b) in enumerate(inputs)]
+    for copy in fetch:
+        copy.start()
     zero3 = jnp.zeros((NX, NY, NZ), F32)
     for bx in range(3):
         for by in range(3):
@@ -423,6 +415,8 @@
         @pl.when(valid(*d))
         def _():
             pl.semaphore_signal(bar, inc=1, device_id=(gx + d[0], gy + d[1]), device_id_type=MESH)
+    fetch[0].wait()
+    fetch[1].wait()
     for x in range(NX):
         rel = (dens[x].astype(F32) + 1.0) / CLASSES
         eb[1, 1, x] = MIN_MODULUS + (1.0 - MIN_MODULUS) * rel * rel * rel
@@ -433,7 +427,7 @@
         halves.append(0.25 * pair_sum(t + pltpu.roll(t, NY - 1, 0), 1))
     e2b[2, 1] = jnp.where((subl() & 1) == 0, halves[0], pltpu.roll(halves[1], 1, 0))
 
-    fetch.wait()
+    fetch[2].wait()
     for c in range(3):
         for x in range(NX):
             for y in range(NY):
@@ -468,6 +462,8 @@
             loadbuf[pl.ds(k * 96 + 64 + i, 4, stride=NC), :] = got[16 * k + 8 : 16 * k + 12]
         return carry
 
+    fetch[3].wait()
+    fetch[4].wait()
     lax.fori_loop(0, NC, load_case, 0)
 
     arrive(K_E, N8, boxes(eb))
@@ -488,9 +484,11 @@
             for j in range(1, 13):
                 k = ((c * 8 + i - 1) * 12 + j - 1) * NC
                 total = fx[i, j] * (raw[c, i, j] + loadbuf[pl.ds(pl.multiple_of(k, NC), NC), :])
-                pending.append((j, jnp.where(ex[i, j] > 0.0, total, 0.0)))
-            for j, val in pending:
+                total = jnp.where(ex[i, j] > 0.0, total, 0.0)
+                pending.append((j, total, ad[c, i, j] * total))
+            for j, val, step in pending:
                 g[0, c, i, j] = val
+                a1[c, i, j] = step
         return carry
 
     lax.fori_loop(1, 9, first_rhs, 0)
@@ -498,14 +496,17 @@
     def unpack(p):
         return jnp.where(even, p, down(p, 1)), jnp.where(even, up(p, 1), p)
 
-    def unpack_field(packed, out, add=None):
+    def unpack_field(packed, out, own, base, add=None):
         for c in range(3):
             for bx in range(3):
                 pending = []
-                for j in range(8):
-                    for a, val in enumerate(unpack(packed[c, bx, j])):
+                for j in range(1 if bx == 0 else 0, 7 if bx == 2 else 8):
+                    inner = bx == 1 and 2 <= j < 6
+                    both = [own[c, base + a, base + j - 2] for a in range(2)] if inner else unpack(packed[c, bx, j])
+                    for a, val in enumerate(both):
                         i = 2 * bx + a
-                        val = jnp.where(ad2[0, i, j] > 0.0, val, 0.0)
+                        if not inner:
+                            val = jnp.where(ad2[0, i, j] > 0.0, val, 0.0)
                         if add is not None:
                             val = val + add[c, i // 2 + 1, j // 2 + 1]
                         pending.append(((c, i, j), val))
@@ -537,21 +538,15 @@
             def clean(i, c2_):
                 for c in range(3):
                     pending = [(j, jnp.where(ex[i, j] > 0.0, rhs[c, i, j], 0.0)) for j in range(1, 13)]
-                    for j, val in pending:
+                    pending = [(j, val, ad[c, i, j] * val) for j, val in pending]
+                    for j, val, step in pending:
                         rhs[c, i, j] = val
+                        a1[c, i, j] = step
                 return c2_
             lax.fori_loop(1, 9, clean, 0)
 
-        def first(i, c2_):
-            for c in range(3):
-                pending = [(j, ad[c, i, j] * rhs[c, i, j]) for j in range(1, 13)]
-                for j, val in pending:
-                    a1[c, i, j] = val
-            return c2_
-
-        lax.fori_loop(1, 9, first, 0)
         smooth(a1, 1, *one_out, co1, w, rhs, bd, a2, 5)
-        restrict(a2, 1, *own, co1, w, rhs, part, t2)
+        restrict(a2, 1, *own, co1, w, rhs, pairs, t2)
         pack_field(t2, (0, 0), g2)
         start(K_G2 + it, N8, coarse_refs(g2))
 
@@ -577,7 +572,7 @@
             )
 
         arrive(K_G2 + it, N8, coarse_refs(g2))
-        unpack_field(g2, g2u)
+        unpack_field(g2, g2u, t2, 0)
         for c in range(3):
             for i in range(6):
                 pending = [(j, ad2[c, i, j] * g2u[c, i, j]) for j in range(8)]
@@ -587,7 +582,7 @@
         smooth(b1, 2, *out2, co2, w2, g2u, bd2, b2, 3)
         pack_field(b2, (2, 2), x2)
         start(K_X2C + it, N8, coarse_refs(x2))
-        restrict(b2, 2, *own2, co2, w2, g2u, part, t3)
+        restrict(b2, 2, *own2, co2, w2, g2u, pairs, t3)
         for c in range(3):
             r0, r1 = t3[c, 0, 0], t3[c, 0, 1]
             s0, s1 = ad3[c, 2, 2] * r0, ad3[c, 2, 3] * r1
@@ -609,13 +604,13 @@
                 ref[idx] = val
         smooth(c1, 4, (1, 4), (1, 5), co3, w3, g3u, bd3, c2, 4)
         arrive(K_X2C + it, N8, coarse_refs(x2))
-        unpack_field(x2, b3, add=c2)
+        unpack_field(x2, b3, b2, 2, add=c2)
         smooth(b3, 2, *out2, co2, w2, g2u, bd2, b4, 3)
         smooth(b4, 2, *own2, co2, w2, g2u, ad2, b1, 4)
         pack_field(b1, (2, 2), ec)
         start(K_EC + it, N8, coarse_refs(ec))
         arrive(K_EC + it, N8, coarse_refs(ec))
-        unpack_field(ec, e2u)
+        unpack_field(ec, e2u, b1, 2)
         arrive(K_X2 + it, N8, x_refs)
 
         def correct(i, from_own):
@@ -712,31 +707,34 @@
             out = out + buffer[k]
         return out
 
-    ps1[gy] = jnp.where(lanes() < 2 * NC, gram[0], pltpu.roll(gram[1], 2 * NC, 1))
+    grams = jnp.where(lanes() < 2 * NC, gram[0], pltpu.roll(gram[1], 2 * NC, 1))
+    folded = jnp.where(lanes() < NZ // 2, grams, pltpu.roll(pltpu.roll(grams, NC // 2, 0), NZ // 2, 1))
+    ps1[gy] = folded[: NC // 2]
     ps2[gx] = total(ps1, gy, size_y, lambda k: (gx, k), 0, settle)
     sums = total(ps2, gx, size_x, lambda k: (k, gy), size_y)
-
-    rz = columns(sums, 0)
-    qp = columns(sums, NC)
-    ru = columns(sums, 2 * NC)
-    qu = columns(sums, 3 * NC)
-    wu = columns(sums, 4 * NC)
-    alpha = solve(qp, rz)
-    alpha_t = flip(alpha)
-    qua = mm(qu, alpha)
-    rz2 = plus(minus(rz, mm(ru, alpha)), mm(alpha_t, minus(qua, qp)))
-    mix = [jnp.where(subl() == k, col + 1.0, col) for k, col in enumerate(solve(rz, rz2))]
-    ahead = minus(mm(flip(qp), mix), qua)
-    behind = minus(mm(flip(wu), alpha), mm(flip(qu), mix))
-    alpha2 = solve(plus(mm(flip(mix), ahead), mm(alpha_t, behind)), rz2)
-    for q, m in enumerate((plus(alpha, mm(mix, alpha2)), mm(alpha, alpha2))):
-        for k, col in enumerate(flip(m)):
+    sums = jnp.concatenate([sums, pltpu.roll(sums, NZ // 2, 1)], axis=0)
+
+    rz = sums
+    qp = up(sums, NC)
+    ru = up(sums, 2 * NC)
+    qu = up(sums, 3 * NC)
+    wu = up(sums, 4 * NC)
+    alpha = solve(columns(qp), rz)
+    alpha_t = flipped(alpha)
+    qua = mm(columns(qu), alpha)
+    rz2 = rz - mm(columns(ru), alpha) + mm(alpha_t, qua - qp)
+    mix = jnp.where(lanes() == subl(), 1.0, 0.0) + solve(columns(rz), rz2)
+    ahead = mm(flipped(qp), mix) - qua
+    behind = mm(flipped(wu), alpha) - mm(flipped(qu), mix)
+    alpha2 = solve(columns(mm(flipped(mix), ahead) + mm(alpha_t, behind)), rz2)
+    for q, m in enumerate((alpha + mm(columns(mix), alpha2), mm(columns(alpha), alpha2))):
+        for k, col in enumerate(flipped(m)):
             mats[q, k] = col
 
     def finish(n, carry):
         c, x = lax.div(n, NX), lax.rem(n, NX)
         i = H + x
-        for one, two, ref, base in ((pv.at[0], pv.at[1], xo, None), (g.at[1], g.at[2], ro, g.at[0])):
+        for one, two, ref, base in ((pv.at[0], pv.at[1], stage.at[0], None), (g.at[1], g.at[2], stage.at[1], g.at[0])):
             accs = [None] * NY
             for k in range(NC):
                 m1, m2 = mats[0, k], mats[1, k]
@@ -749,7 +747,16 @@
                 ref[pl.ds((c * NC * NX + x) * NY + y, NC, stride=NX * NY), :] = val
         return carry
 
-    lax.fori_loop(0, 3 * NX, finish, 0)
+    stores = []
+    for c in range(3):
+        lax.fori_loop(c * NX, (c + 1) * NX, finish, 0)
+        part = pl.ds(c * NC * NX * NY, NC * NX * NY)
+        for q, ref in enumerate((xo, ro)):
+            copy = pltpu.make_async_copy(stage.at[q, part], ref.at[part], stored.at[q, c])
+            copy.start()
+            stores.append(copy)
+    for copy in stores:
+        copy.wait()
 
 
 def publish(a, b, out_a, out_b, stage, sem):
@@ -770,7 +777,7 @@
 
 
 def on_device(size_x, size_y, source_field, density_class, fixed_mask, load_nodes, load_forces):
-    rows = 3 * NC * NX * NY
+    rows = NROWS
     tile = (NC, NZ)
 
     def vm(*dims):
@@ -783,31 +790,34 @@
         pltpu.VMEM((3, 3, NX, NY, NZ), F32), pltpu.VMEM((3, 3, NX, NY, NZ), F32), vm(5, 3),
         vm(AX, AY), vm(AX, AY), vm(10, 12), vm(5, 6), vm(),
         vm(3, 3, AX, AY), vm(2, 3, AX, AY), vm(3, AX, AY), vm(3, AX, AY), vm(3, AX, AY), vm(3, AX, AY),
-        vm(2, 3, AX, AY), vm(AX, AY), pltpu.VMEM((3 * 8 * 12 * NC, NZ), F32),
+        vm(2, 3, AX, AY), vm(AX, AY), pltpu.VMEM((3 * 8 * 12 * NC + 4 * NC, NZ), F32),
     ]
     scratch += level(AX, AY) + level(6, 8) + level(5, 6)
     scratch += [vm(3, 2, 4), vm(2, 3, 3, 8), vm(2, 3, 3, 8), vm(2, 3, 3, 8)]
     scratch += [vm(3, 6, 8)] * 5 + [vm(6, 8), vm(3, 6, 8)]
     scratch += [vm(3, 1, 2), vm(2, 3, 5, 3), vm(3, 5, 6), vm(3, 5, 6), vm(3, 5, 6), vm(5, 6)]
-    scratch += [vm(2), vm(size_y), vm(size_x), vm(2, NC), vm(3, AX, AY), vm(3, NX, 4)]
+    half = (NC // 2, NZ)
+    scratch += [vm(2), pltpu.VMEM((size_y,) + half, F32), pltpu.VMEM((size_x,) + half, F32), vm(2, NC), vm(3, AX, AY), vm(3, NX, 4)]
     scratch += [pltpu.VMEM((AX, 16, NZ), F32)] * 2
     sems = pltpu.SemaphoreType.DMA
     scratch += [sems((KINDS, len(N14))), sems((KINDS, len(N14))), sems((size_x + size_y,)), sems((size_x + size_y,))]
-    scratch += [pltpu.VMEM((rows, NZ), F32), sems(())]
-    spec = pl.BlockSpec(memory_space=pltpu.VMEM)
+    spare = NROWS + NX * NY
+    scratch += [pltpu.VMEM((spare, NZ), F32), pltpu.VMEM((2, spare, NZ), F32), sems((2, 3))]
+    scratch += [pltpu.VMEM(v.shape, v.dtype) for v in (density_class, fixed_mask, load_nodes, load_forces)]
+    scratch += [sems((5,))]
+    whole = pl.BlockSpec(memory_space=pl.ANY)
     shape = jax.ShapeDtypeStruct((rows, NZ), F32)
     sol, res = pl.pallas_call(
         functools.partial(kernel, size_x, size_y),
         out_shape=(shape, shape),
-        in_specs=[pl.BlockSpec(memory_space=pl.ANY)] + [spec] * 4,
-        out_specs=(spec, spec),
+        in_specs=[whole] * 5,
+        out_specs=(whole, whole),
         scratch_shapes=scratch,
         compiler_params=pltpu.CompilerParams(
             collective_id=0, has_side_effects=True, vmem_limit_bytes=56 * 1024 * 1024
         ),
         name="block_pcg",
     )(source_field.reshape(rows, NZ), density_class, fixed_mask, load_nodes, load_forces)
-    whole = pl.BlockSpec(memory_space=pl.ANY)
     sol, res = pl.pallas_call(
         publish,
         out_shape=(shape, shape),

time: 107 us -> 106 us (level)
    pallas_call x1, Pallas kernels: 104 us -> 103 us  [on_device(): pl.pallas_call(functools.partial(kernel, size_x, size_y), out_shape=(shap...]
where the time goes in v4:
time: 106 us
  Pallas kernels  105 us (99%)
    pallas_call x1, Pallas kernels, on_device(): pl.pallas_call(functools.partial(kernel, size_x, size_y), out_shape=(shap...  103 us

profile of v4, /device:TPU:1, one launch (start us, length us, event | category | flops | bytes accessed | tf_op | source)
XLA Modules:
  0.0 105.6 jit_solution(14039604980037043951)
XLA Ops:
  0.6 102.9 %block_pcg.1 = (f32[768,128]{1,0:T(8,128)}, f32[768,128]{1,0:T(8,128)}) custom-call(f32[768,128]{1,0:T(8,128)} %bitcast.3, s32[4,8,128]{2,1,0:T(8,128)} %dens_in.1, s32[4,8,128]{2,1,0:T(8,128)} %mask_in.1, s32[8,64]{1,0:T(8,128)} %nodes_in.1, f32[3,8,64]{2,1,0:T(8,128)} %forces_in.1), custom_call_target="tpu_custom_call" | custom-call | tf_op jit(solution)/shard_map/block_pcg/pallas_call | solution.py:810
  103.6 2.0 %publish.1 = (f32[768,128]{1,0:T(8,128)}, f32[768,128]{1,0:T(8,128)}) custom-call(f32[768,128]{1,0:T(8,128)} %get-tuple-element.6.a, f32[768,128]{1,0:T(8,128)} %get-tuple-element.7.b), custom_call_target="tpu_custom_call" | custom-call | tf_op jit(solution)/shard_map/publish/pallas_call | solution.py:821

commit v5 on v4

--- a/solution.py
+++ b/solution.py
@@ -496,7 +496,7 @@
     def unpack(p):
         return jnp.where(even, p, down(p, 1)), jnp.where(even, up(p, 1), p)
 
-    def unpack_field(packed, out, own, base, add=None):
+    def unpack_field(packed, out, own, base):
         for c in range(3):
             for bx in range(3):
                 pending = []
@@ -507,8 +507,6 @@
                         i = 2 * bx + a
                         if not inner:
                             val = jnp.where(ad2[0, i, j] > 0.0, val, 0.0)
-                        if add is not None:
-                            val = val + add[c, i // 2 + 1, j // 2 + 1]
                         pending.append(((c, i, j), val))
                 for idx, val in pending:
                     out[idx] = val
@@ -589,6 +587,8 @@
             g3[c, 2, 1] = jnp.where(low2, jnp.where(even, r0, r1), jnp.where(even, s0, s1))
         start(K_G3 + it, N14, g3_refs(g3))
         start(K_X2 + it, N8, x_refs)
+        arrive(K_X2C + it, N8, coarse_refs(x2))
+        unpack_field(x2, b3, b2, 2)
         arrive(K_G3 + it, N14, g3_refs(g3))
         for c in range(3):
             pending = []
@@ -603,8 +603,16 @@
             for ref, idx, val in pending:
                 ref[idx] = val
         smooth(c1, 4, (1, 4), (1, 5), co3, w3, g3u, bd3, c2, 4)
-        arrive(K_X2C + it, N8, coarse_refs(x2))
-        unpack_field(x2, b3, b2, 2, add=c2)
+
+        def add_coarsest(n, c2_):
+            c, i = lax.div(n, 6), lax.rem(n, 6)
+            at = lax.div(i, 2) + 1
+            pending = [(j, b3[c, i, j] + c2[c, at, j // 2 + 1]) for j in range(8)]
+            for j, val in pending:
+                b3[c, i, j] = val
+            return c2_
+
+        lax.fori_loop(0, 18, add_coarsest, 0)
         smooth(b3, 2, *out2, co2, w2, g2u, bd2, b4, 3)
         smooth(b4, 2, *own2, co2, w2, g2u, ad2, b1, 4)
         pack_field(b1, (2, 2), ec)

time: 106 us -> 106 us (level)
  no operation moved by 1% of the time
where the time goes in v5:
time: 106 us
  Pallas kernels  105 us (99%)
    pallas_call x1, Pallas kernels, on_device(): pl.pallas_call(functools.partial(kernel, size_x, size_y), out_shape=(shap...  103 us

profile of v5, /device:TPU:1, one launch (start us, length us, event | category | flops | bytes accessed | tf_op | source)
XLA Modules:
  0.0 105.9 jit_solution(3419521946646682171)
XLA Ops:
  0.6 103.3 %block_pcg.1 = (f32[768,128]{1,0:T(8,128)}, f32[768,128]{1,0:T(8,128)}) custom-call(f32[768,128]{1,0:T(8,128)} %bitcast.3, s32[4,8,128]{2,1,0:T(8,128)} %dens_in.1, s32[4,8,128]{2,1,0:T(8,128)} %mask_in.1, s32[8,64]{1,0:T(8,128)} %nodes_in.1, f32[3,8,64]{2,1,0:T(8,128)} %forces_in.1), custom_call_target="tpu_custom_call" | custom-call | tf_op jit(solution)/shard_map/block_pcg/pallas_call | solution.py:818
  103.9 2.0 %publish.1 = (f32[768,128]{1,0:T(8,128)}, f32[768,128]{1,0:T(8,128)}) custom-call(f32[768,128]{1,0:T(8,128)} %get-tuple-element.6.a, f32[768,128]{1,0:T(8,128)} %get-tuple-element.7.b), custom_call_target="tpu_custom_call" | custom-call | tf_op jit(solution)/shard_map/publish/pallas_call | solution.py:829
